TPU v7x, 128 devices: a whole 4x4x4 slice. The times are simulated.
128 devices in a mesh: row: 8 (over z_lo, y), col: 16 (over z_hi, x, core).
Axes of the slice: x: 4, y: 4, z: 4 (z_hi: 2, z_lo: 2; z = z_hi * 2 + z_lo), core: 2. Of those that a mesh axis runs over, the one named last changes fastest.
Arguments:
- features: bfloat16 [16, 6144, 128], P('col', 'row'), may hold values from -6 to 6
- tile_values: bfloat16 [8, 16, 96, 128, 128], P('row', 'col'), may hold values from -0.1875 to 0.1875
- tile_rows: int32 [8, 16, 96], P('row', 'col'), may hold values from 0 to 95
- tile_cols: int32 [8, 16, 96], P('row', 'col'), may hold values from 0 to 47
- tile_counts: int32 [8, 16], P('row', 'col'), may hold values from 24 to 96, as said below
- in_weight: bfloat16 [128, 256], replicated, may hold values from -0.5 to 0.5
- out_weight: bfloat16 [256, 172], replicated, may hold values from -0.375 to 0.375
- labels: int32 [8, 12288], P('row', 'col'), may hold values from 0 to 171
- loss_mask: int32 [8, 12288], P('row', 'col'), may hold values 0 or 1
Outputs:
- total_loss: float32 [], replicated
- grad_in: float32 [128, 256], replicated
- grad_out: float32 [256, 172], replicated
- grad_features: float32 [16, 6144, 128], P('col', 'row')
Inputs may be any that keep to these rules, and one draw needn't show every extreme that they name: `tile_counts`: slots below a device's count are live, the rest are ignored; some device has all 96 slots live.
All inputs are finite; a program needn't handle non-finite values. No bound on the sum of `loss_mask` on one device may be relied on, other than what follows from the above.
Results may differ from a plain program's by a relative error of at most 0.0038.
The roundings to bfloat16 on the way count: a program that leaves them out, or rounds other values in their place, can miss the bound.
Values may be sent and summed in bfloat16 or wider, within the bound.
A program may use at most 128 MiB of HBM per device.

v0:
```python
import jax
import jax.numpy as jnp
from jax import lax
from jax.sharding import PartitionSpec as P


def dense_head(rows_sum, node_labels, node_mask, in_weight, out_weight, count_sum):
    rounded_rows = rows_sum.astype(jnp.bfloat16)
    pre_act = jnp.dot(rounded_rows, in_weight, preferred_element_type=jnp.float32)
    sig_act = jax.nn.sigmoid(pre_act)
    hidden = (pre_act * sig_act).astype(jnp.bfloat16)
    logits = jnp.dot(hidden, out_weight, preferred_element_type=jnp.float32)
    log_norm = jnp.log(jnp.sum(jnp.exp(logits), axis=-1))
    onehot = (
        node_labels[:, None] == jnp.arange(out_weight.shape[1], dtype=jnp.int32)[None, :]
    ).astype(jnp.float32)
    weights_row = node_mask.astype(jnp.float32)
    counted = count_sum(jnp.sum(weights_row))
    loss_part = jnp.sum(weights_row * (log_norm - jnp.sum(logits * onehot, axis=-1))) / counted
    log_grad = (
        (weights_row / counted)[:, None] * (jnp.exp(logits - log_norm[:, None]) - onehot)
    ).astype(jnp.bfloat16)
    grad_out = lax.dot_general(
        hidden, log_grad, (((0,), (0,)), ((), ())), preferred_element_type=jnp.float32
    )
    grad_hidden = lax.dot_general(
        log_grad, out_weight, (((1,), (1,)), ((), ())), preferred_element_type=jnp.float32
    )
    grad_pre = (grad_hidden * sig_act * (1.0 + pre_act * (1.0 - sig_act))).astype(jnp.bfloat16)
    grad_in = lax.dot_general(
        rounded_rows, grad_pre, (((0,), (0,)), ((), ())), preferred_element_type=jnp.float32
    )
    grad_feed = lax.dot_general(
        grad_pre, in_weight, (((1,), (1,)), ((), ())), preferred_element_type=jnp.float32
    )
    return (loss_part, grad_in, grad_out, grad_feed.astype(jnp.bfloat16))


def count_block(value):
    return lax.psum(value, "row")


def shards(
    features,
    tile_values,
    tile_rows,
    tile_cols,
    tile_counts,
    in_weight,
    out_weight,
    labels,
    loss_mask,
):
    tile_size = tile_values.shape[-1]
    in_width = features.shape[-1]
    slot_count = tile_values.shape[2]
    values = tile_values[0, 0]
    live_slots = (jnp.arange(slot_count, dtype=jnp.int32) < tile_counts[0, 0]).astype(jnp.float32)[
        :, None, None
    ]
    feature_rows = lax.all_gather(features, "row", axis=1, tiled=True)[0]
    col_tiles = feature_rows.shape[0] // tile_size
    row_tiles = labels.shape[1] * lax.axis_size("col") // tile_size
    picked = feature_rows.reshape(col_tiles, tile_size, in_width)[tile_cols[0, 0]]
    product = (
        jnp.einsum("tab,tbf->taf", values, picked, preferred_element_type=jnp.float32) * live_slots
    )
    partial_value = jax.ops.segment_sum(product, tile_rows[0, 0], num_segments=row_tiles).reshape(
        row_tiles * tile_size, in_width
    )
    summed = lax.psum(partial_value, "col")
    block_labels, block_mask = (
        lax.all_gather(labels, "col", axis=1, tiled=True),
        lax.all_gather(loss_mask, "col", axis=1, tiled=True),
    )
    loss_part, grad_in, grad_out, grad_feed = dense_head(
        summed, block_labels[0], block_mask[0], in_weight, out_weight, count_block
    )
    total_loss, grad_in, grad_out = lax.psum((loss_part, grad_in, grad_out), "row")
    grad_tiles = grad_feed.reshape(row_tiles, tile_size, in_width)[tile_rows[0, 0]]
    back_product = (
        jnp.einsum("tab,taf->tbf", values, grad_tiles, preferred_element_type=jnp.float32)
        * live_slots
    )
    column_part = jax.ops.segment_sum(
        back_product, tile_cols[0, 0], num_segments=col_tiles
    ).reshape(col_tiles * tile_size, in_width)
    grad_features = lax.psum_scatter(column_part, "row", scatter_dimension=0, tiled=True)
    return (total_loss, grad_in, grad_out, grad_features[None])


def solution(mesh):
    placed = (
        P("col", "row", None),
        P("row", "col", None, None, None),
        P("row", "col", None),
        P("row", "col", None),
        P("row", "col"),
        P(),
        P(),
        P("row", "col"),
        P("row", "col"),
    )
    return jax.shard_map(
        shards,
        mesh=mesh,
        in_specs=placed,
        out_specs=(P(), P(), P(), P("col", "row", None)),
        check_vma=False,
    )
```

profile of v0, /device:TPU:0, one launch (start us, length us, event | category | flops | bytes accessed | tf_op | source)
XLA Modules:
  0.0 380.4 jit_solution(15309307160074341892)
XLA Ops:
  7.2 0.7 all-gather.2.cloned.1.call-update
  8.0 25.6 %all_gather.9 = s32[1,12288]{1,0:T(1,128)S(1)} all-gather(s32[1,768]{1,0:T(1,128)} %param.17), channel_id=1, replica_groups=mesh['row'=8,'col'=16] {'col'}, dimensions={1}, use_global_device_ids=true | all-gather | bytes 52224 | tf_op jit(solution)/shard_map/all_gather | solution.py:74
  33.6 0.7 convert_reduce_fusion
  34.3 20.1 %psum.36 = f32[]{:T(128)} all-reduce(f32[]{:T(128)} %convert_reduce_fusion), channel_id=1, replica_groups=mesh['row'=8,'col'=16] {'row'}, use_global_device_ids=true, to_apply=%region_6.0 | all-reduce | flops 1 | bytes 8 | tf_op jit(solution)/shard_map/psum | solution.py:40
  55.1 19.4 %all_gather.11 = s32[1,12288]{1,0:T(1,128)S(1)} all-gather(s32[1,768]{1,0:T(1,128)} %param.16), channel_id=1, replica_groups=mesh['row'=8,'col'=16] {'col'}, dimensions={1}, use_global_device_ids=true | all-gather | bytes 52224 | tf_op jit(solution)/shard_map/all_gather | solution.py:73
  74.4 0.7 fusion.14
  75.1 0.7 fusion.15
  75.8 4.1 %gather_fusion = bf16[96,128,128]{2,1,0:T(8,128)(2,1)} fusion(bf16[48,128,128]{2,1,0:T(8,128)(2,1)} %bitcast.47, s32[1024]{0:T(1024)S(1)} %pad_clamp_fusion.1), kind=kCustom, calls=%fused_computation | custom fusion | bytes 6291840 | tf_op jit(solution)/shard_map/gather | solution.py:64
  79.9 6.9 %multiply_bitcast_fusion.1 = f32[96,128,128]{1,2,0:T(8,128)} fusion(f32[96]{0:T(128)S(1)} %compare_convert_fusion, bf16[96,128,128]{2,1,0:T(8,128)(2,1)} %gather_fusion, bf16[1,1,96,128,128]{4,3,2,1,0:T(8,128)(2,1)S(1)} %copy-done), kind=kOutput, calls=%fused_computation.15 | convolution fusion | flops 404226048 | bytes 12583296 | tf_op jit(solution)/shard_map/tab,tbf->taf/dot_general | solution.py:66
  86.8 6.6 %copy.16 = f32[96,128,128]{2,1,0:T(8,128)} copy(f32[96,128,128]{1,2,0:T(8,128)} %multiply_bitcast_fusion.1) | data formatting | bytes 12582912 | tf_op jit(solution)/shard_map/mul | solution.py:66
  93.4 3.4 broadcast_in_dim.6
  96.9 20.2 %scatter_fusion = f32[96,128,128]{2,1,0:T(8,128)} fusion(f32[96,128,128]{2,1,0:T(8,128)} %broadcast_in_dim.6, s32[96]{0:T(128)S(1)} %bitcast.52, f32[96,128,128]{2,1,0:T(8,128)} %copy.16), kind=kCustom, calls=%fused_computation.2 | custom fusion | flops 1572864 | bytes 18874752 | tf_op jit(solution)/shard_map/scatter-add | solution.py:68
  117.1 97.7 %all-reduce.5 = bf16[12288,128]{1,0:T(8,128)(2,1)} all-reduce(f32[12288,128]{1,0:T(8,128)} %bitcast.44), channel_id=1, replica_groups=mesh['row'=8,'col'=16] {'col'}, use_global_device_ids=true, to_apply=%region_1.0 | all-reduce | flops 1572864 | bytes 9437184 | tf_op jit(solution)/shard_map/psum | solution.py:71
  214.8 8.2 %multiply_convert_fusion = (bf16[12288,256]{1,0:T(8,128)(2,1)S(1)}, f32[12288,256]{1,0:T(8,128)}) fusion(bf16[12288,128]{1,0:T(8,128)(2,1)} %all-reduce.5, bf16[128,256]{1,0:T(8,128)(2,1)S(1)} %copy-done.3), kind=kOutput, calls=%fused_computation.8 | convolution fusion | flops 821035008 | bytes 22085632 | tf_op jit(solution)/shard_map/dot_general | solution.py:9
  223.0 2.9 exponential_reduce_fusion
  226.0 1.8 broadcast_divide_fusion
  227.7 2.8 fusion.16
  230.6 11.5 %fusion.1 = bf16[12288,256]{1,0:T(8,128)(2,1)S(1)} fusion(bf16[256,172]{0,1:T(8,128)(2,1)S(1)} %copy-done.6, f32[12288,256]{1,0:T(8,128)} %get-tuple-element.12, f32[12288,172]{0,1:T(8,128)} %copy-done.7, f32[12288]{0:T(1024)S(1)} %get-tuple-element.10, f32[12288]{0:T(1024)S(1)} %get-tuple-element.8, s32[12288]{0:T(1024)S(1)} %bitcast.51), kind=kOutput, calls=%fused_computation.6 | convolution fusion | flops 1123123200 | bytes 27564032 | tf_op jit(solution)/shard_map/dot_general | solution.py:26
  242.1 2.7 copy-done.1
  244.7 1.9 fusion.17
  246.6 6.3 %convolution_convert_fusion = bf16[12288,128]{1,0:T(8,128)(2,1)} fusion(bf16[12288,256]{1,0:T(8,128)(2,1)} %copy-done.1, bf16[128,256]{1,0:T(8,128)(2,1)S(1)} %copy-done.3), kind=kOutput, calls=%fused_computation.7 | convolution fusion | flops 806879232 | bytes 9502720 | tf_op jit(solution)/shard_map/dot_general | solution.py:33
  252.9 0.3 reduce-scatter.2.cloned.1.call-start
  253.2 4.6 %gather_fusion.1 = bf16[96,128,128]{2,1,0:T(8,128)(2,1)} fusion(bf16[96,128,128]{2,1,0:T(8,128)(2,1)} %bitcast.46, s32[1024]{0:T(1024)S(1)} %pad_clamp_fusion), kind=kCustom, calls=%fused_computation.1 | custom fusion | bytes 6291840 | tf_op jit(solution)/shard_map/gather | solution.py:80
  257.8 6.1 %multiply_bitcast_fusion = f32[96,128,128]{1,2,0:T(8,128)} fusion(f32[96]{0:T(128)S(1)} %compare_convert_fusion, bf16[96,128,128]{2,1,0:T(8,128)(2,1)} %gather_fusion.1, bf16[1,1,96,128,128]{4,3,2,1,0:T(8,128)(2,1)S(1)} %copy-done), kind=kOutput, calls=%fused_computation.14 | convolution fusion | flops 404226048 | bytes 12583296 | tf_op jit(solution)/shard_map/tab,taf->tbf/dot_general | solution.py:82
  263.9 6.6 %copy.18 = f32[96,128,128]{2,1,0:T(8,128)} copy(f32[96,128,128]{1,2,0:T(8,128)} %multiply_bitcast_fusion) | data formatting | bytes 12582912 | tf_op jit(solution)/shard_map/mul | solution.py:82
  270.5 2.1 broadcast_in_dim.7
  272.6 19.9 %scatter_fusion.1 = f32[48,128,128]{2,1,0:T(8,128)} fusion(f32[48,128,128]{2,1,0:T(8,128)} %broadcast_in_dim.7, s32[96]{0:T(128)S(1)} %bitcast.53, f32[96,128,128]{2,1,0:T(8,128)} %copy.18), kind=kCustom, calls=%fused_computation.3 | custom fusion | flops 1572864 | bytes 18874752 | tf_op jit(solution)/shard_map/scatter-add | solution.py:85
  293.8 16.5 %psum.37 = f32[]{:T(128)} all-reduce(f32[]{:T(128)S(6)} %div.17), channel_id=1, replica_groups=mesh['row'=8,'col'=16] {'row'}, use_global_device_ids=true, to_apply=%region_7.0 | all-reduce | flops 1 | bytes 8 | tf_op jit(solution)/shard_map/psum | solution.py:79
  310.3 12.1 %all-reduce.4.cloned.1.call-done = (f32[128,256]{1,0:T(8,128)}, f32[256,172]{0,1:T(8,128)}) async-done(((f32[128,256]{1,0:T(8,128)}, f32[256,172]{0,1:T(8,128)}), (f32[128,256]{1,0:T(8,128)}, f32[256,172]{0,1:T(8,128)})) %all-reduce.4.cloned.1.call-update) | async-done | bytes 307216 | tf_op jit(solution)/shard_map/psum | solution.py:79
  322.3 48.4 %reduce-scatter.2.cloned.1.call-done = f32[768,128]{1,0:T(8,128)} async-done(((f32[6144,128]{1,0:T(8,128)}), f32[768,128]{1,0:T(8,128)}) %reduce-scatter.2.cloned.1.call-update) | async-done | bytes 393232 | tf_op jit(solution)/shard_map/reduce_scatter | solution.py:88
  370.7 1.6 copy.28
  372.3 1.6 copy.29
  (24 shorter events, 0.2 us)
Async XLA Ops:
  7.2 72.8 %copy-start = (bf16[1,1,96,128,128]{4,3,2,1,0:T(8,128)(2,1)S(1)}, bf16[1,1,96,128,128]{4,3,2,1,0:T(8,128)(2,1)}, u32[]{:S(2)}) copy-start(bf16[1,1,96,128,128]{4,3,2,1,0:T(8,128)(2,1)} %param.10) | copy-start | bytes 9437188
  7.2 68.6 %all-gather.2.cloned.1.call-start = ((), (), s32[]{:S(2)}) async-start(), calls=%async_computation.1 | async-start | bytes 1769472 | tf_op jit(solution)/shard_map/all_gather | solution.py:61
  7.9 314.4 %all-reduce.4.cloned.1.call-start = ((), (), s32[]{:S(2)}) async-start(), calls=%async_computation.3 | async-start | bytes 622592 | tf_op jit(solution)/shard_map/psum | solution.py:79
  93.4 3.4 copy-start.4
  117.1 97.7 %copy-start.3 = (bf16[128,256]{1,0:T(8,128)(2,1)S(1)}, bf16[128,256]{1,0:T(8,128)(2,1)}, u32[]{:S(2)}) copy-start(bf16[128,256]{1,0:T(8,128)(2,1)} %param.14) | copy-start | bytes 196612
  214.8 8.2 %copy-start.6 = (bf16[256,172]{0,1:T(8,128)(2,1)S(1)}, bf16[256,172]{0,1:T(8,128)(2,1)}, u32[]{:S(2)}) copy-start(bf16[256,172]{0,1:T(8,128)(2,1)} %param.15) | copy-start | bytes 264196
  226.0 4.6 %copy-start.7 = (f32[12288,172]{0,1:T(8,128)}, f32[12288,172]{0,1:T(8,128)S(1)}, u32[]{:S(2)}) copy-start(f32[12288,172]{0,1:T(8,128)S(1)} %get-tuple-element.13) | copy-start | bytes 25362436
  230.6 14.2 %copy-start.2 = (bf16[12288,128]{1,0:T(8,128)(2,1)S(1)}, bf16[12288,128]{1,0:T(8,128)(2,1)}, u32[]{:S(2)}) copy-start(bf16[12288,128]{1,0:T(8,128)(2,1)} %all-reduce.5) | copy-start | bytes 9437188
  242.1 2.7 copy-start.1
  252.9 117.8 %reduce-scatter.2.cloned.1.call-start = ((), (), s32[]{:S(2)}) async-start(), calls=%async_computation.2 | async-start | bytes 3538944 | tf_op jit(solution)/shard_map/reduce_scatter | solution.py:88
  263.9 8.7 %copy-start.5 = (s32[1,1,96]{2,1,0:T(1,128)S(1)}, s32[1,1,96]{2,1,0:T(1,128)}, u32[]{:S(2)}) copy-start(s32[1,1,96]{2,1,0:T(1,128)} %param.12) | copy-start | bytes 1156
Sparse Core Ops, SparseCore 0:
  9.7 43.0 all-gather.1
  253.0 69.2 all-reduce.3
  325.5 45.1 reduce-scatter.1
where the time goes:
time: 381 us; the launch traced here: 380 us
  blocking collectives  179 us (47%)
  waiting for transfers between devices  61.2 us (16%)
  matrix products  46.6 us (12%)
  other arithmetic  43.9 us (12%)
  local copies, waits for them, and re-layouts  33.3 us (9%)
  between operations  15.8 us (4%)
    psum x1, blocking collectives, shards(): summed = lax.psum(partial_value, 'col')  97.7 us
    reduce_scatter x1, waiting for transfers between devices, shards(): lax.psum_scatter(column_part, 'row', scatter_dimension=0, tiled=True)  48.4 us
    all_gather x1, blocking collectives, shards(): lax.all_gather(loss_mask, 'col', axis=1, tiled=True)  25.6 us
    scatter-add x1, other arithmetic, shards(): jax.ops.segment_sum(product, tile_rows[0, 0], num_segments=row_tiles)  20.2 us
    psum x1, blocking collectives, count_block(): return lax.psum(value, 'row')  20.1 us
    scatter-add x1, other arithmetic, shards(): jax.ops.segment_sum(back_product, tile_cols[0, 0], num_segments=col_tiles)  19.9 us
    all_gather x1, blocking collectives, shards(): lax.all_gather(labels, 'col', axis=1, tiled=True)  19.4 us
    psum x1, blocking collectives, shards(): lax.psum((loss_part, grad_in, grad_out), 'row')  16.5 us
  transfers between devices with their start and end apart: 3, of which 2 were waited for; matrix products, arithmetic and copies ran while one was open for 11% of the time, Pallas kernels for 0%

commit v1 on v0

v1 whole, which is shorter than its diff:
```python
import functools

import jax
import jax.numpy as jnp
from jax import lax
from jax.experimental import pallas as pl
from jax.experimental.pallas import tpu as pltpu
from jax.sharding import PartitionSpec as P

F32, BF16, I32 = jnp.float32, jnp.bfloat16, jnp.int32
TILE = 128
SLOTS = 96
ROW_TILES = 96
COL_TILES = 48
OWN = 6
HALF = 3
CLS = 172
HID = 256
UNROLL = 8
N_SEMS = 112
WIRE2 = (BF16, BF16, BF16, BF16, BF16, BF16, F32)
WIRE4 = (BF16, BF16, BF16, BF16, BF16, BF16, F32)


def gather_blocks(copy, buf, block, ring, pair, first_src, work, landed):
    def part(dr, dp, half):
        return buf.at[pl.ds(block(dr, dp) * OWN + half * HALF, HALF)]

    def send(dr, dp, half, to):
        src = part(dr, dp, half)
        if (dr, dp) == (0, 0):
            src = first_src(half)
        c = copy(src, part(dr, dp, half), to)
        c.start()
        return c

    up, down, across = ring(1), ring(-1), pair
    own_up = {0: send(0, 0, 0, up)}
    own_down = {1: send(0, 0, 1, down)}
    own_pair = {0: send(0, 0, 0, across)}
    own_pair[1] = send(0, 0, 1, across)
    own_up[1] = send(0, 0, 1, up)
    own_down[0] = send(0, 0, 0, down)
    work(0)
    sends = [*own_up.values(), *own_down.values(), *own_pair.values()]
    own_up[0].wait_recv()
    far0 = send(-1, 0, 0, up)
    landed(-1, 0, 0)
    own_down[1].wait_recv()
    far1 = send(1, 0, 1, down)
    landed(1, 0, 1)
    work(1)
    beside = {}
    for half in (0, 1):
        own_pair[half].wait_recv()
        beside[0, half] = send(0, 1, half, up)
        beside[1, half] = send(0, 1, half, down)
        landed(0, 1, half)
    work(2)
    own_up[1].wait_recv()
    landed(-1, 0, 1)
    own_down[0].wait_recv()
    landed(1, 0, 0)
    far0.wait_recv()
    last0 = send(2, 0, 0, across)
    landed(2, 0, 0)
    far1.wait_recv()
    last1 = send(2, 0, 1, across)
    landed(2, 0, 1)
    work(3)
    for half in (0, 1):
        beside[0, half].wait_recv()
        landed(-1, 1, half)
        beside[1, half].wait_recv()
        landed(1, 1, half)
    last0.wait_recv()
    landed(2, 1, 0)
    last1.wait_recv()
    landed(2, 1, 1)
    return sends + [far0, far1, *beside.values(), last0, last1]


def scatter_blocks(copy, out, inn, ring, pair, source, work):
    up, down, across = ring(1), ring(-1), pair

    def halves(half):
        return pl.ds(half * HALF, HALF)

    def fill(slot, half, chip, *received):
        local = source(*chip)

        @pl.loop(half * HALF, half * HALF + HALF)
        def _(t):
            value = local(t)
            for n in received:
                value = value + inn[n][t].astype(F32)
            out[slot][t] = value.astype(out[slot].dtype)

    def send(slot, half, to, recv_slot):
        c = copy(out[slot].at[halves(half)], inn[recv_slot].at[halves(half)], to)
        c.start()
        return c

    z_far = []
    for half in (0, 1):
        fill(0, half, (2, 1))
        z_far.append(send(0, half, across, 0))
    x_up, x_down = [], []
    for half in (0, 1):
        fill(1, half, (1, 1))
        x_up.append(send(1, half, up, 1))
        fill(2, half, (-1, 1))
        x_down.append(send(2, half, down, 2))
    fill(3, 1, (1, 0))
    up_hi = send(3, 1, up, 3)
    fill(4, 0, (-1, 0))
    down_lo = send(4, 0, down, 4)
    work(0)
    z_far[0].wait_recv()
    fill(5, 0, (2, 0), 0)
    far_up = send(5, 0, up, 5)
    z_far[1].wait_recv()
    fill(5, 1, (2, 0), 0)
    far_down = send(5, 1, down, 5)
    work(1)
    z_near = []
    for half in (0, 1):
        x_up[half].wait_recv()
        x_down[half].wait_recv()
        fill(6, half, (0, 1), 1, 2)
        z_near.append(send(6, half, across, 6))
    far_up.wait_recv()
    fill(3, 0, (1, 0), 5)
    up_lo = send(3, 0, up, 3)
    far_down.wait_recv()
    fill(4, 1, (-1, 0), 5)
    down_hi = send(4, 1, down, 4)
    work(2)
    up_hi.wait_recv()
    down_lo.wait_recv()
    z_near[0].wait_recv()
    z_near[1].wait_recv()
    up_lo.wait_recv()
    down_hi.wait_recv()

    local = source(0, 0)

    def total(t):
        return local(t) + inn[3][t].astype(F32) + inn[4][t].astype(F32) + inn[6][t].astype(F32)

    return total, [*z_far, *x_up, *x_down, up_hi, down_lo, far_up, far_down, *z_near, up_lo, down_hi]


def order_slots(key, other, live, slots, tiles, idx, base):
    sub = lax.broadcasted_iota(I32, (slots, slots), 0)
    lane = lax.broadcasted_iota(I32, (slots, slots), 1)
    diag = sub == lane

    def column(v):
        return jnp.sum(jnp.where(diag, jnp.broadcast_to(v, (slots, slots)), 0), axis=1, keepdims=True)

    lane1 = lax.broadcasted_iota(I32, (1, slots), 1)
    sort_l = jnp.where(live > 0, key * TILE + lane1, tiles * TILE + lane1)
    sort_c, key_c, other_c, live_c = column(sort_l), column(key), column(other), column(live)
    rank_c = jnp.sum((jnp.broadcast_to(sort_l, (slots, slots)) < sort_c).astype(I32), axis=1, keepdims=True)

    def place(v):
        return jnp.sum(jnp.where(rank_c == lane, v, 0), axis=0, keepdims=True)

    idx[base : base + 1, 0:slots] = place(sub)
    idx[base + 1 : base + 2, 0:slots] = place(other_c)
    idx[base + 2 : base + 3, 0:slots] = place(key_c)
    below = jnp.sum(jnp.where(key_c <= lane, live_c, 0), axis=0, keepdims=True)
    same = jnp.sum(jnp.where(key_c == lane, live_c, 0), axis=0, keepdims=True)
    idx[base + 3 : base + 4, 0:slots] = jnp.maximum(below - 1, 0)
    idx[base + 4 : base + 5, 0:slots] = same


def tile_products(left, right, sums, where, base):
    def step(i, acc):
        for u in range(UNROLL):
            k = i * UNROLL + u
            prod = jnp.dot(left[where[base, k]], right[where[base + 1, k]], preferred_element_type=F32)
            before = jnp.maximum(k - 1, 0)
            keep = (where[base + 2, k] == where[base + 2, before]).astype(F32)
            acc = jnp.where(keep > 0, acc, 0.0) + prod
            sums[k] = acc
        return acc

    lax.fori_loop(0, SLOTS // UNROLL, step, jnp.zeros((TILE, TILE), F32))


def kernel(
    feat, vals_hbm, trow, tcol, tcnt, win, wout, lab, msk,
    loss_o, gin_o, gout_o, gf_o,
    vals, vals_t, feats, sums, core_out, core_in, *rest):
    out2, in2, out4, in4, rest = rest[0:7], rest[7:14], rest[14:21], rest[21:28], rest[28:]
    (grads,
    idx, where, lab_c, msk_c, wpad, rows_s, hid_s, lgrad_s, pre_s, gin_s, gout_s,
    m_part, y_in, m_y, x_in, z_all, c_out, c_in, final,
    cnt_out, cnt_in, send_sem, recv_sem, local_sem) = rest
    row, col = lax.axis_index("row"), lax.axis_index("col")
    zl, y = row // 4, row % 4
    zh, x, k = col // 8, (col // 2) % 4, col % 2

    def chip(zl_=zl, y_=y, zh_=zh, x_=x, k_=k):
        return {"row": zl_ * 4 + y_, "col": (zh_ * 4 + x_) * 2 + k_}

    def y_at(d):
        return chip(y_=(y + d + 4) % 4)

    def x_at(d):
        return chip(x_=(x + d + 4) % 4)

    z_others = [chip(zl_=1 - zl), chip(zh_=1 - zh), chip(zl_=1 - zl, zh_=1 - zh)]
    y_others = [y_at(d) for d in (1, 2, 3)]
    x_others = [x_at(d) for d in (1, 2, 3)]
    y_pair, x_pair, core = chip(zl_=1 - zl), chip(zh_=1 - zh), chip(k_=1 - k)

    used = []

    def copy(src, dst, to):
        n = len(used)
        used.append(n)
        return pltpu.make_async_remote_copy(
            src_ref=src, dst_ref=dst, send_sem=send_sem.at[n], recv_sem=recv_sem.at[n],
            device_id=to, device_id_type=pl.DeviceIdType.MESH,
        )

    def sent(src, dst, to):
        c = copy(src, dst, to)
        c.start()
        return c

    open_sends = []

    load_vals = pltpu.make_async_copy(vals_hbm.at[0, 0], vals, local_sem.at[0])
    load_vals.start()
    load_own = pltpu.make_async_copy(feat, feats.at[pl.ds(row * OWN, OWN)], local_sem.at[1])
    load_own.start()

    partners = [*y_others, *x_others, *z_others, core]
    barrier = pltpu.get_barrier_semaphore()
    for p in partners:
        pl.semaphore_signal(barrier, inc=1, device_id=p, device_id_type=pl.DeviceIdType.MESH)
    pl.semaphore_wait(barrier, len(partners))

    count_groups = [y_others, x_others, z_others, [core]]
    count_copies = []

    def count_send(stage):
        count_copies.append(
            [sent(cnt_out.at[stage], cnt_in.at[stage, n], to) for n, to in enumerate(count_groups[stage])]
        )

    def count_take(stage):
        for c in count_copies[stage]:
            c.wait_recv()
        value = cnt_out[stage]
        for n in range(len(count_groups[stage])):
            value = value + cnt_in[stage, n]
        cnt_out[stage + 1] = value

    def transpose(first, last):
        @pl.loop(first, last)
        def _(s):
            vals_t[s] = vals[s].astype(F32).T.astype(BF16)

    def prepare():
        slot = lax.broadcasted_iota(I32, (1, SLOTS), 1)
        live = (slot < tcnt[...]).astype(I32)
        idx[...] = jnp.zeros(idx.shape, I32)
        order_slots(trow[0], tcol[0], live, SLOTS, ROW_TILES, idx, 0)
        order_slots(tcol[0], trow[0], live, SLOTS, ROW_TILES, idx, 5)
        to_smem = pltpu.make_async_copy(idx, where, local_sem.at[2])
        to_smem.start()
        to_smem.wait()
        sub = lax.broadcasted_iota(I32, (TILE, TILE), 0)
        lane = lax.broadcasted_iota(I32, (TILE, TILE), 1)
        for t in range(OWN):
            for ref, dst in ((lab, lab_c), (msk, msk_c)):
                line = jnp.broadcast_to(ref[:, t * TILE : (t + 1) * TILE], (TILE, TILE))
                dst[t] = jnp.broadcast_to(
                    jnp.sum(jnp.where(sub == lane, line, 0), axis=1, keepdims=True), (TILE, TILE)
                )
        wpad[...] = jnp.zeros(wpad.shape, BF16)
        wpad[0:CLS] = wout[...]

    def work1(stage):
        if stage == 0:
            cnt_out[0] = jnp.broadcast_to(jnp.sum(msk[...].astype(F32), axis=1, keepdims=True), (8, TILE))
            count_send(0)
            prepare()
            load_vals.wait()
        elif stage == 1:
            transpose(0, 8)
        elif stage == 2:
            count_take(0)
            count_send(1)
            transpose(8, 16)
        else:
            transpose(16, 24)
            count_take(1)
            count_send(2)

    open_sends += gather_blocks(
        copy, feats, lambda dr, dp: (zl + dp) % 2 * 4 + (y + dr + 4) % 4, y_at, y_pair,
        lambda half: feat.at[pl.ds(half * HALF, HALF)], work1, lambda dr, dp, half: None,
    )
    load_own.wait()

    tile_products(vals, feats, sums, where, 0)

    def row_sum(tile):
        return sums[where[3, tile]] * (where[4, tile] > 0).astype(F32)

    def col_sum(tile):
        return sums[where[8, tile]] * (where[9, tile] > 0).astype(F32)

    def chip_index(dr, dp):
        return (zh + dp) % 2 * 4 + (x + dr + 4) % 4

    classes = [(2, 1), (1, 1), (-1, 1), (1, 0), (-1, 0), (2, 0), (0, 1), (0, 0)]
    core_copies = {}
    for n, (dr, dp) in enumerate(classes):
        base = (chip_index(dr, dp) * 2 + 1 - k) * OWN

        @pl.loop(0, OWN)
        def _(t, n=n, base=base):
            core_out[n, t] = row_sum(base + t)

        core_copies[dr, dp] = sent(core_out.at[n], core_in.at[n], core)
    taken = set()

    def source2(dr, dp):
        if (dr, dp) not in taken:
            taken.add((dr, dp))
            core_copies[dr, dp].wait_recv()
        base = (chip_index(dr, dp) * 2 + k) * OWN
        return lambda t: row_sum(base + t) + core_in[classes.index((dr, dp)), t]

    def work2(stage):
        if stage == 0:
            transpose(24, 40)
        elif stage == 1:
            count_take(2)
            count_send(3)
            transpose(40, 56)
        else:
            transpose(56, 76)
            count_take(3)

    total2, sends2 = scatter_blocks(copy, out2, in2, x_at, x_pair, source2, work2)
    open_sends += [*sends2, *core_copies.values()]

    counted = cnt_out[4][0:1, 0:1]
    lane = lax.broadcasted_iota(I32, (TILE, HID), 1)

    def head(t, loss):
        rounded = total2(t).astype(BF16)
        rows_s[t] = rounded
        pre = jnp.dot(rounded, win[...], preferred_element_type=F32)
        sig = jax.nn.sigmoid(pre)
        hidden = (pre * sig).astype(BF16)
        hid_s[t] = hidden
        logits = lax.dot_general(hidden, wpad[...], (((1,), (1,)), ((), ())), preferred_element_type=F32)
        log_norm = jnp.log(jnp.sum(jnp.where(lane < CLS, jnp.exp(logits), 0.0), axis=1, keepdims=True))
        onehot = (lane == lab_c[t][:, 0:1]).astype(F32)
        weight = msk_c[t][:, 0:1].astype(F32)
        loss = loss + weight * (log_norm - jnp.sum(logits * onehot, axis=1, keepdims=True))
        prob = jnp.where(lane < CLS, jnp.exp(logits - log_norm), 0.0)
        log_grad = ((weight / counted) * (prob - onehot)).astype(BF16)
        lgrad_s[t] = log_grad
        back = jnp.dot(log_grad, wpad[...], preferred_element_type=F32)
        grad_pre = (back * sig * (1.0 + pre * (1.0 - sig))).astype(BF16)
        pre_s[t] = grad_pre
        feed = lax.dot_general(grad_pre, win[...], (((1,), (1,)), ((), ())), preferred_element_type=F32)
        grads[col * OWN + t] = feed.astype(BF16)
        return loss

    loss = lax.fori_loop(0, OWN, head, jnp.zeros((TILE, 1), F32))
    loss = jnp.sum(loss, axis=0, keepdims=True) / counted

    steps = {}

    def weight_grads():
        over = (((0,), (0,)), ((), ()))
        gin_s[...] = jnp.zeros((TILE, HID), F32)
        gout_s[...] = jnp.zeros((HID, HID), F32)

        @pl.loop(0, OWN)
        def _(t):
            gin_s[...] += lax.dot_general(rows_s[t], pre_s[t], over, preferred_element_type=F32)
            gout_s[...] += lax.dot_general(lgrad_s[t], hid_s[t], over, preferred_element_type=F32)

        sub = lax.broadcasted_iota(I32, (8, HID), 0)
        lane = lax.broadcasted_iota(I32, (8, HID), 1)
        gout_s[HID - 8 : HID] = jnp.where((sub == 7) & (lane == 0), jnp.broadcast_to(loss, (8, HID)), gout_s[HID - 8 : HID])
        for n in range(16):
            for r in range(0, 24, 8):
                at = n * 24 + r
                m_part[n // 4, n % 4, r : r + 8] = gin_s[at : at + 8] if at < TILE else gout_s[at - TILE : at - TILE + 8]
        steps["y"] = [
            sent(m_part.at[(y + d) % 4], y_in.at[d - 1], to) for d, to in zip((1, 2, 3), y_others)
        ]

    def sum_y():
        for c in steps["y"]:
            c.wait_recv()
        for n in range(4):
            m_y[n] = m_part[y, n] + y_in[0, n] + y_in[1, n] + y_in[2, n]
        steps["x"] = [sent(m_y.at[(x + d) % 4], x_in.at[d - 1], to) for d, to in zip((1, 2, 3), x_others)]

    def sum_x():
        for c in steps["x"]:
            c.wait_recv()
        me = zh * 2 + zl
        z_all[me] = m_y[x] + x_in[0] + x_in[1] + x_in[2]
        steps["z"] = [sent(z_all.at[me], z_all.at[me], to) for to in z_others]

    def sum_z():
        for c in steps["z"]:
            c.wait_recv()
        c_out[...] = (z_all[0] + z_all[1]) + (z_all[2] + z_all[3])
        steps["core"] = [sent(c_out, c_in, core)]

    def sum_core():
        for c in steps["core"]:
            c.wait_recv()
        final[x, y] = c_out[...] + c_in[...]
        steps["spread_y"] = [sent(final.at[x, y], final.at[x, y], to) for to in y_others]

    def spread_x():
        for c in steps["spread_y"]:
            c.wait_recv()
        steps["spread_x"] = [sent(final.at[x], final.at[x], to) for to in x_others]

    hand_over = []

    def hand(dr, dp, half):
        at = pl.ds((chip_index(dr, dp) * 2 + k) * OWN + half * HALF, HALF)
        hand_over.append(sent(grads.at[at], grads.at[at], core))

    def work3(stage):
        if stage == 0:
            for half in (0, 1):
                hand(0, 0, half)
            weight_grads()
            transpose(76, 86)
        elif stage == 1:
            transpose(86, 96)
        elif stage == 3:
            sum_y()

    open_sends += gather_blocks(
        copy, grads, lambda dr, dp: chip_index(dr, dp) * 2 + k, x_at, x_pair,
        lambda half: grads.at[pl.ds(col * OWN + half * HALF, HALF)], work3, hand,
    )
    for c in hand_over:
        c.wait_recv()
    open_sends += hand_over

    tile_products(vals_t, grads, sums, where, 5)

    def source4(dr, dp):
        base = ((zl + dp) % 2 * 4 + (y + dr + 4) % 4) * OWN
        return lambda t: col_sum(base + t)

    def work4(stage):
        if stage == 0:
            sum_x()
        elif stage == 1:
            sum_z()
            sum_core()
        else:
            spread_x()

    total4, sends4 = scatter_blocks(copy, out4, in4, y_at, y_pair, source4, work4)
    open_sends += sends4

    @pl.loop(0, OWN)
    def _(t):
        gf_o[t] = total4(t)

    for c in steps["spread_x"]:
        c.wait_recv()
    for n in range(16):
        for r in range(0, 24, 8):
            at = n * 24 + r
            piece = final[n % 4, n // 4, r : r + 8]
            if at < TILE:
                gin_o[at : at + 8] = piece
            else:
                put = min(8, CLS - (at - TILE))
                if put > 0:
                    gout_o[at - TILE : at - TILE + put] = piece[0:put]
                if at == TILE + HID - 8:
                    loss_o[...] = jnp.broadcast_to(piece[7:8, 0:1], loss_o.shape)

    for group in steps.values():
        open_sends += group
    for group in count_copies:
        open_sends += group
    for c in open_sends:
        c.wait_send()


def hand_out(loss, gin, gout, gf, loss_o, gin_o, gout_o, gf_o):
    loss_o[0] = loss[0, 0]
    gin_o[...] = gin[...]
    gout_o[...] = gout[...]
    gf_o[...] = gf[...]


def shards(
    features,
    tile_values,
    tile_rows,
    tile_cols,
    tile_counts,
    in_weight,
    out_weight,
    labels,
    loss_mask,
):
    vmem = pl.BlockSpec(memory_space=pltpu.VMEM)
    smem = pl.BlockSpec(memory_space=pltpu.SMEM)
    hbm = pl.BlockSpec(memory_space=pl.ANY)
    block = (OWN, TILE, TILE)
    loss, grad_in, grad_out, grad_features = pl.pallas_call(
        kernel,
        out_shape=(
            jax.ShapeDtypeStruct((8, TILE), F32),
            jax.ShapeDtypeStruct((TILE, HID), F32),
            jax.ShapeDtypeStruct((CLS, HID), F32),
            jax.ShapeDtypeStruct(block, F32),
        ),
        in_specs=[hbm, hbm, vmem, vmem, vmem, vmem, vmem, vmem, vmem],
        out_specs=(vmem, vmem, vmem, vmem),
        scratch_shapes=[
            pltpu.VMEM((SLOTS, TILE, TILE), BF16),
            pltpu.VMEM((SLOTS, TILE, TILE), BF16),
            pltpu.VMEM((COL_TILES, TILE, TILE), BF16),
            pltpu.VMEM((SLOTS, TILE, TILE), F32),
            pltpu.VMEM((8, *block), F32),
            pltpu.VMEM((8, *block), F32),
            *(pltpu.VMEM(block, wire) for kinds in (WIRE2, WIRE2, WIRE4, WIRE4) for wire in kinds),
            pltpu.VMEM((ROW_TILES, TILE, TILE), BF16),
            pltpu.VMEM((16, TILE), I32),
            pltpu.SMEM((16, TILE), I32),
            pltpu.VMEM(block, I32),
            pltpu.VMEM(block, I32),
            pltpu.VMEM((HID, HID), BF16),
            pltpu.VMEM((OWN, TILE, TILE), BF16),
            pltpu.VMEM((OWN, TILE, HID), BF16),
            pltpu.VMEM((OWN, TILE, HID), BF16),
            pltpu.VMEM((OWN, TILE, HID), BF16),
            pltpu.VMEM((TILE, HID), F32),
            pltpu.VMEM((HID, HID), F32),
            pltpu.VMEM((4, 4, 24, HID), F32),
            pltpu.VMEM((3, 4, 24, HID), F32),
            pltpu.VMEM((4, 24, HID), F32),
            pltpu.VMEM((3, 24, HID), F32),
            pltpu.VMEM((4, 24, HID), F32),
            pltpu.VMEM((24, HID), F32),
            pltpu.VMEM((24, HID), F32),
            pltpu.VMEM((4, 4, 24, HID), F32),
            pltpu.VMEM((5, 8, TILE), F32),
            pltpu.VMEM((4, 3, 8, TILE), F32),
            pltpu.SemaphoreType.DMA((N_SEMS,)),
            pltpu.SemaphoreType.DMA((N_SEMS,)),
            pltpu.SemaphoreType.DMA((3,)),
        ],
        compiler_params=pltpu.CompilerParams(
            collective_id=0, has_side_effects=True, vmem_limit_bytes=56 * 1024 * 1024
        ),
        name="graph_layer",
    )(
        features.reshape(OWN, TILE, TILE),
        tile_values,
        tile_rows[0],
        tile_cols[0],
        tile_counts,
        in_weight,
        out_weight.T,
        labels,
        loss_mask,
    )
    shapes = (loss, grad_in, grad_out, grad_features)
    loss, grad_in, grad_out, grad_features = pl.pallas_call(
        hand_out,
        out_shape=(jax.ShapeDtypeStruct((1,), F32), *(jax.ShapeDtypeStruct(s.shape, F32) for s in shapes[1:])),
        in_specs=[vmem] * 4,
        out_specs=(smem, vmem, vmem, vmem),
        name="hand_out",
    )(*shapes)
    return loss.reshape(()), grad_in, grad_out.T, grad_features.reshape(1, OWN * TILE, TILE)


def solution(mesh):
    placed = (
        P("col", "row", None),
        P("row", "col", None, None, None),
        P("row", "col", None),
        P("row", "col", None),
        P("row", "col"),
        P(),
        P(),
        P("row", "col"),
        P("row", "col"),
    )
    return jax.shard_map(
        shards,
        mesh=mesh,
        in_specs=placed,
        out_specs=(P(), P(), P(), P("col", "row", None)),
        check_vma=False,
    )
```

time: 381 us -> 94.6 us (0.25)
  blocking collectives: 179 us -> 0 us
  Pallas kernels: 0 us -> 92.9 us
  waiting for transfers between devices: 61.2 us -> 0 us
  matrix products: 46.6 us -> 0 us
  other arithmetic: 43.9 us -> 0 us
  local copies, waits for them, and re-layouts: 33.3 us -> 0 us
  between operations: 15.8 us -> 1.29 us
    psum x3 -> x0, blocking collectives: 134 us -> none  [the longest x1 97.7 us: shards(): summed = lax.psum(partial_value, 'col')]
    pallas_call x0 -> x2, Pallas kernels: none -> 92.9 us  [the longest x1 90.8 us: shards(): pl.pallas_call(kernel, out_shape=(jax.ShapeDtypeStruct((8, TILE), F32), j...]
    reduce_scatter x1 -> x0, waiting for transfers between devices: 48.4 us -> none  [shards(): lax.psum_scatter(column_part, 'row', scatter_dimension=0, tiled=True)]
    dot_general x8 -> x0, matrix products: 46.6 us -> none  [the longest x1 11.5 us: dense_head(): lax.dot_general(log_grad, out_weight, (((1,), (1,)), ((), ())), preferred...]
    all_gather x2 -> x0, blocking collectives: 45 us -> none  [the longest x1 25.6 us: shards(): lax.all_gather(loss_mask, 'col', axis=1, tiled=True)]
    scatter-add x2 -> x0, other arithmetic: 40.1 us -> none  [the longest x1 20.2 us: shards(): jax.ops.segment_sum(product, tile_rows[0, 0], num_segments=row_tiles)]
    mul x2 -> x0, local copies, waits for them, and re-layouts: 13.2 us -> none  [the longest x1 6.62 us: shards(): jnp.einsum('tab,taf->tbf', values, grad_tiles, preferred_element_type=jnp...]
    psum x1 -> x0, waiting for transfers between devices: 12.1 us -> none  [shards(): lax.psum((loss_part, grad_in, grad_out), 'row')]
  transfers between devices with their start and end apart: 3 -> 0, of which waited for: 2 -> 0; matrix products, arithmetic and copies ran while one was open for 11% -> 0% of each run, Pallas kernels for 0% -> 0%
where the time goes in v1:
time: 94.6 us; the launch traced here: 94.2 us
  Pallas kernels  92.9 us (98%)
  between operations  1.29 us (1%)
    pallas_call x1, Pallas kernels, shards(): pl.pallas_call(kernel, out_shape=(jax.ShapeDtypeStruct((8, TILE), F32), j...  90.8 us
    pallas_call x1, Pallas kernels, shards(): pl.pallas_call(hand_out, out_shape=(jax.ShapeDtypeStruct((1,), F32), *(ja...  2.03 us

profile of v1, /device:TPU:0, one launch (start us, length us, event | category | flops | bytes accessed | tf_op | source)
XLA Modules:
  0.0 94.2 jit_solution(12640163105845798677)
XLA Ops:
  1.3 90.8 %graph_layer.1 = (f32[8,128]{1,0:T(8,128)}, f32[128,256]{1,0:T(8,128)}, f32[172,256]{1,0:T(8,128)}, f32[6,128,128]{2,1,0:T(8,128)}) custom-call(bf16[6,128,128]{2,1,0:T(8,128)(2,1)} %bitcast.7, bf16[1,1,96,128,128]{4,3,2,1,0:T(8,128)(2,1)} %vals_hbm.1, s32[1,96]{1,0:T(1,128)} %bitcast.9, s32[1,96]{1,0:T(1,128)} %bitcast.10, s32[1,1]{1,0:T(1,128)S(6)} %copy.13.tcnt, ...), custom_call_target="tpu_custom_call" | custom-call | tf_op jit(solution)/shard_map/graph_layer/pallas_call | solution.py:530
  92.1 2.0 %hand_out.1 = (f32[1]{0:T(128)}, f32[128,256]{1,0:T(8,128)}, f32[172,256]{1,0:T(8,128)}, f32[6,128,128]{2,1,0:T(8,128)}) custom-call(f32[8,128]{1,0:T(8,128)} %get-tuple-element.12.loss, f32[128,256]{1,0:T(8,128)} %get-tuple-element.13.gin, f32[172,256]{1,0:T(8,128)} %get-tuple-element.14.gout, f32[6,128,128]{2,1,0:T(8,128)} %get-tuple-element.15.gf), custom_call_target="tpu_custom_call" | custom-call | tf_op jit(solution)/shard_map/hand_out/pallas_call | solution.py:590

commit v2 on v0

v2 whole, which is shorter than its diff:
```python
import jax
import jax.numpy as jnp
from jax import lax
from jax.experimental import pallas as pl
from jax.experimental.pallas import tpu as pltpu
from jax.sharding import PartitionSpec as P

F32, BF16, I32 = jnp.float32, jnp.bfloat16, jnp.int32
TILE = 128
WIDE = 64
SLOTS = 96
ROW_TILES = 96
COL_TILES = 48
OWN = 6
HALF = 3
CLS = 172
CLS_ROWS = 176
HID = 256
UNROLL = 48
N_SEMS = 184
MESSAGES = ("far_pair", "side_up", "side_down", "free_up", "free_down", "far", "near_pair", "late_up", "late_down")
WIRE2 = (BF16, BF16, BF16, BF16, BF16, BF16, F32, F32, F32)
WIRE4 = (BF16, BF16, BF16, BF16, BF16, BF16, BF16, BF16, BF16)
NT = (((1,), (1,)), ((), ()))


def gather(copy, buf, block, ring, pair, landed):
    def send(dr, dp, half, to):
        at = buf.at[pl.ds(block(dr, dp) * OWN + half * HALF, HALF)]
        return copy(at, at, to)

    up, down, across = ring(1), ring(-1), pair
    up0, down1, pair0 = send(0, 0, 0, up), send(0, 0, 1, down), send(0, 0, 0, across)
    up1, down0, pair1 = send(0, 0, 1, up), send(0, 0, 0, down), send(0, 0, 1, across)
    yield "own"
    for c in (up0, down1, pair0, up1, down0, pair1):
        c.wait_send()
    yield "left"
    up0.wait_recv()
    far0 = send(-1, 0, 0, up)
    landed(-1, 0, 0)
    down1.wait_recv()
    far1 = send(1, 0, 1, down)
    landed(1, 0, 1)
    yield "far"
    beside = []
    for half, c in enumerate((pair0, pair1)):
        c.wait_recv()
        beside.append((send(0, 1, half, up), send(0, 1, half, down)))
        landed(0, 1, half)
    yield "beside"
    up1.wait_recv()
    landed(-1, 0, 1)
    down0.wait_recv()
    landed(1, 0, 0)
    far0.wait_recv()
    last0 = send(2, 0, 0, across)
    landed(2, 0, 0)
    far1.wait_recv()
    last1 = send(2, 0, 1, across)
    landed(2, 0, 1)
    yield "last"
    for half in (0, 1):
        beside[half][0].wait_recv()
        landed(-1, 1, half)
        beside[half][1].wait_recv()
        landed(1, 1, half)
    last0.wait_recv()
    landed(2, 1, 0)
    last1.wait_recv()
    landed(2, 1, 1)
    yield "done"


def scatter(copy, out, inn, chunk, ring, pair, source, result):
    up, down, across = ring(1), ring(-1), pair
    both = (0, OWN)
    halves = ((0, HALF), (HALF, OWN))

    def fill(name, span, chip, *received):
        local = source(*chip)
        ref = out[name]

        for t in range(*span):
            value = local(t)
            for n in received:
                value = value + inn[n][chunk, t].astype(F32)
            ref[chunk, t] = value.astype(ref.dtype)

    def send(name, span, to):
        at = pl.ds(span[0], span[1] - span[0])
        return copy(out[name].at[chunk, at], inn[name].at[chunk, at], to)

    far_pair = []
    for span in halves:
        fill("far_pair", span, (2, 1))
        far_pair.append(send("far_pair", span, across))
    fill("side_up", both, (1, 1))
    side_up = send("side_up", both, up)
    fill("side_down", both, (-1, 1))
    side_down = send("side_down", both, down)
    fill("free_up", halves[1], (1, 0))
    free_up = send("free_up", halves[1], up)
    fill("free_down", halves[0], (-1, 0))
    free_down = send("free_down", halves[0], down)
    yield "start"
    far_pair[0].wait_recv()
    fill("far", halves[0], (2, 0), "far_pair")
    far_up = send("far", halves[0], up)
    far_pair[1].wait_recv()
    fill("far", halves[1], (2, 0), "far_pair")
    far_down = send("far", halves[1], down)
    yield "far"
    side_up.wait_recv()
    side_down.wait_recv()
    near = []
    for span in halves:
        fill("near_pair", span, (0, 1), "side_up", "side_down")
        near.append(send("near_pair", span, across))
    yield "near"
    far_up.wait_recv()
    fill("late_up", halves[0], (1, 0), "far")
    late_up = send("late_up", halves[0], up)
    far_down.wait_recv()
    fill("late_down", halves[1], (-1, 0), "far")
    late_down = send("late_down", halves[1], down)
    yield "late"
    for c in (free_up, free_down, near[0], near[1], late_up, late_down):
        c.wait_recv()
    local = source(0, 0)
    for t in range(OWN):
        from_below = inn["late_up" if t < HALF else "free_up"][chunk, t]
        from_above = inn["free_down" if t < HALF else "late_down"][chunk, t]
        value = local(t) + from_below.astype(F32) + from_above.astype(F32)
        result(t, value + inn["near_pair"][chunk, t].astype(F32))
    yield "done"


def order_slots(key, other, live, slots, tiles, idx, base):
    sub = lax.broadcasted_iota(I32, (slots, slots), 0)
    lane = lax.broadcasted_iota(I32, (slots, slots), 1)
    diag = sub == lane

    def column(v):
        return jnp.sum(jnp.where(diag, jnp.broadcast_to(v, (slots, slots)), 0), axis=1, keepdims=True)

    lane1 = lax.broadcasted_iota(I32, (1, slots), 1)
    sort_l = jnp.where(live > 0, key * TILE + lane1, tiles * TILE + lane1)
    sort_c, key_c, other_c, live_c = column(sort_l), column(key), column(other), column(live)
    rank_c = jnp.sum((jnp.broadcast_to(sort_l, (slots, slots)) < sort_c).astype(I32), axis=1, keepdims=True)

    def place(v):
        return jnp.sum(jnp.where(rank_c == lane, v, 0), axis=0, keepdims=True)

    idx[base : base + 1, 0:slots] = place(sub)
    idx[base + 1 : base + 2, 0:slots] = place(other_c)
    idx[base + 2 : base + 3, 0:slots] = place(key_c)
    below = jnp.sum(jnp.where(key_c <= lane, live_c, 0), axis=0, keepdims=True)
    same = jnp.sum(jnp.where(key_c == lane, live_c, 0), axis=0, keepdims=True)
    idx[base + 3 : base + 4, 0:slots] = jnp.maximum(below - 1, 0)
    idx[base + 4 : base + 5, 0:slots] = same


def tile_products(product, sums, where, base):
    def step(i, acc):
        for u in range(UNROLL):
            k = i * UNROLL + u
            prod = product(where[base, k], where[base + 1, k])
            keep = where[base + 2, k] == where[base + 2, jnp.maximum(k - 1, 0)]
            acc = jnp.where(keep, acc, 0.0) + prod
            sums[k] = acc
        return acc

    lax.fori_loop(0, SLOTS // UNROLL, step, jnp.zeros((WIDE, TILE), F32))


class Copy:
    def __init__(self, src, dst, to, send_sem, recv_sem):
        self.copy = pltpu.make_async_remote_copy(
            src_ref=src, dst_ref=dst, send_sem=send_sem, recv_sem=recv_sem,
            device_id=to, device_id_type=pl.DeviceIdType.MESH,
        )
        self.sending = True
        self.copy.start()

    def wait_recv(self):
        self.copy.wait_recv()

    def wait_send(self):
        if self.sending:
            self.sending = False
            self.copy.wait_send()


def run_to(phase, step):
    while next(phase) != step:
        pass


def kernel(
    feat, vals_hbm, trow_h, tcol_h, tcnt_h, win_h, wout_h, lab_h, msk_h,
    loss_o, gin_o, gout_o, gf_o,
    trow, tcol, tcnt, win, wout, lab, msk,
    feat_v, vals, vals_t, xt_a, xt_b, gt_a, gt_b, sums, core_out, core_in, gf_t,
    idx, where, win_t, wpad, wpad_t, rows_s, hid_s, lgrad_s, pre_s, gin_s, gout_s,
    m_part, y_in, m_y, x_in, z_all, c_out, c_in, final,
    cnt_out, cnt_in, send_sem, recv_sem, local_sem, *messages,
):
    row, col = lax.axis_index("row"), lax.axis_index("col")
    zl, y = row // 4, row % 4
    zh, x, k = col // 8, (col // 2) % 4, col % 2
    xt, gt = (xt_a, xt_b), (gt_a, gt_b)
    out2, in2, out4, in4 = (dict(zip(MESSAGES, messages[n : n + 9])) for n in (0, 9, 18, 27))

    def chip(zl_=zl, y_=y, zh_=zh, x_=x, k_=k):
        return {"row": zl_ * 4 + y_, "col": (zh_ * 4 + x_) * 2 + k_}

    def y_at(d):
        return chip(y_=(y + d + 4) % 4)

    def x_at(d):
        return chip(x_=(x + d + 4) % 4)

    def row_chip(dr, dp):
        return (zl + dp) % 2 * 4 + (y + dr + 4) % 4

    def col_chip(dr, dp):
        return (zh + dp) % 2 * 4 + (x + dr + 4) % 4

    z_others = [chip(zl_=1 - zl), chip(zh_=1 - zh), chip(zl_=1 - zl, zh_=1 - zh)]
    y_others = [y_at(d) for d in (1, 2, 3)]
    x_others = [x_at(d) for d in (1, 2, 3)]
    y_pair, x_pair, core = chip(zl_=1 - zl), chip(zh_=1 - zh), chip(k_=1 - k)

    copies = []

    def copy(src, dst, to):
        n = len(copies)
        copies.append(Copy(src, dst, to, send_sem.at[n], recv_sem.at[n]))
        return copies[n]

    load_own = pltpu.make_async_copy(feat, feat_v, local_sem.at[0])
    load_own.start()
    load_vals = pltpu.make_async_copy(vals_hbm.at[0, 0], vals, local_sem.at[1])
    load_vals.start()
    pairs = ((trow_h, trow), (tcol_h, tcol), (tcnt_h, tcnt), (win_h, win), (wout_h, wout), (lab_h, lab), (msk_h, msk))
    loads = [pltpu.make_async_copy(src, dst, local_sem.at[3 + n]) for n, (src, dst) in enumerate(pairs)]
    for c in loads:
        c.start()

    partners = [*y_others, *x_others, *z_others, core]
    barrier = pltpu.get_barrier_semaphore()
    for p in partners:
        pl.semaphore_signal(barrier, inc=1, device_id=p, device_id_type=pl.DeviceIdType.MESH)
    load_own.wait()
    for t in range(OWN):
        turned = feat_v[t].astype(F32).T.astype(BF16)
        xt_a[row * OWN + t] = turned[0:WIDE]
        xt_b[row * OWN + t] = turned[WIDE:]
    pl.semaphore_wait(barrier, len(partners))

    count_groups = [y_others, x_others, z_others, [core]]
    count_copies = []

    def count_send(stage):
        count_copies.append(
            [copy(cnt_out.at[stage], cnt_in.at[stage, n], to) for n, to in enumerate(count_groups[stage])]
        )

    def count_take(stage):
        for c in count_copies[stage]:
            c.wait_recv()
        value = cnt_out[stage]
        for n in range(len(count_groups[stage])):
            value = value + cnt_in[stage, n]
        cnt_out[stage + 1] = value

    def prepare_slots():
        slot = lax.broadcasted_iota(I32, (1, SLOTS), 1)
        live = (slot < tcnt[...]).astype(I32)
        idx[...] = jnp.zeros(idx.shape, I32)
        order_slots(trow[...], tcol[...], live, SLOTS, ROW_TILES, idx, 0)
        order_slots(tcol[...], trow[...], live, SLOTS, ROW_TILES, idx, 5)
        to_smem = pltpu.make_async_copy(idx, where, local_sem.at[2])
        to_smem.start()
        to_smem.wait()

    def prepare_weights():
        win_t[...] = win[...].astype(F32).T.astype(BF16)
        wpad[...] = jnp.zeros(wpad.shape, BF16)
        wpad[0:CLS] = wout[...]
        wpad_t[...] = wpad[...].astype(F32).T.astype(BF16)
        lgrad_s[...] = jnp.zeros(lgrad_s.shape, BF16)

    def row_sum(chunk, tile):
        return sums[chunk, where[3, tile]] * (where[4, tile] > 0).astype(F32)

    def col_sum(chunk, tile):
        return sums[chunk, where[8, tile]] * (where[9, tile] > 0).astype(F32)

    def forward(chunk):
        def product(slot, other):
            return jnp.dot(xt[chunk][other], vals_t[slot], preferred_element_type=F32)

        tile_products(product, sums.at[chunk], where, 0)

    def backward(chunk):
        def product(slot, other):
            return jnp.dot(gt[chunk][other], vals[slot], preferred_element_type=F32)

        tile_products(product, sums.at[chunk], where, 5)

    classes = [(2, 1), (1, 1), (-1, 1), (1, 0), (-1, 0), (2, 0), (0, 1), (0, 0)]
    core_copies = {}

    def core_send(chunk):
        for n, (dr, dp) in enumerate(classes):
            base = (col_chip(dr, dp) * 2 + 1 - k) * OWN
            for t in range(OWN):
                core_out[chunk, n, t] = row_sum(chunk, base + t)
            core_copies[chunk, dr, dp] = copy(core_out.at[chunk, n], core_in.at[chunk, n], core)

    def forward_source(chunk):
        taken = set()

        def source(dr, dp):
            if (dr, dp) not in taken:
                taken.add((dr, dp))
                core_copies[chunk, dr, dp].wait_recv()
            base, n = (col_chip(dr, dp) * 2 + k) * OWN, classes.index((dr, dp))
            return lambda t: row_sum(chunk, base + t) + core_in[chunk, n, t]

        return source

    def take_rows(chunk):
        def result(t, value):
            lanes = slice(t % 2 * TILE, t % 2 * TILE + TILE)
            rows_s[t // 2, chunk * WIDE : chunk * WIDE + WIDE, lanes] = value.astype(BF16)

        return result

    gather_a, gather_b = (
        gather(copy, xt[c], row_chip, y_at, y_pair, lambda dr, dp, half: None) for c in (0, 1)
    )
    scatter_a, scatter_b = (
        scatter(copy, out2, in2, c, x_at, x_pair, forward_source(c), take_rows(c)) for c in (0, 1)
    )
    run_to(gather_a, "own")
    for c in loads:
        c.wait()
    cnt_out[0] = jnp.broadcast_to(jnp.sum(msk[...].astype(F32), axis=1, keepdims=True), (8, TILE))
    count_send(0)
    run_to(gather_a, "left")
    run_to(gather_b, "own")
    prepare_slots()
    run_to(gather_a, "beside")
    run_to(gather_b, "far")
    count_take(0)
    count_send(1)
    run_to(gather_a, "last")
    run_to(gather_b, "beside")
    prepare_weights()
    load_vals.wait()

    @pl.loop(0, SLOTS, unroll=8)
    def _(n):
        vals_t[n] = vals[n].T

    run_to(gather_b, "last")
    run_to(gather_a, "done")
    forward(0)
    core_send(0)
    count_take(1)
    count_send(2)
    run_to(gather_b, "done")
    forward(1)
    core_send(1)
    run_to(scatter_a, "start")
    run_to(scatter_b, "start")
    run_to(scatter_a, "far")
    run_to(scatter_a, "near")
    count_take(2)
    count_send(3)
    run_to(scatter_b, "far")
    run_to(scatter_a, "late")
    run_to(scatter_b, "near")
    run_to(scatter_b, "late")
    count_take(3)
    run_to(scatter_a, "done")
    run_to(scatter_b, "done")

    counted = cnt_out[4][0:1, 0:1]
    sub = lax.broadcasted_iota(I32, (CLS_ROWS, 2 * TILE), 0)
    loss = jnp.zeros((1, 2 * TILE), F32)
    for j in range(OWN // 2):
        nodes = slice(j * 2 * TILE, (j + 1) * 2 * TILE)
        pre = jnp.dot(win_t[...], rows_s[j], preferred_element_type=F32)
        sig = jax.nn.sigmoid(pre)
        hidden = (pre * sig).astype(BF16)
        hid_s[j] = hidden
        logits = jnp.dot(wpad[0:CLS_ROWS], hidden, preferred_element_type=F32)
        log_norm = jnp.log(jnp.sum(jnp.where(sub < CLS, jnp.exp(logits), 0.0), axis=0, keepdims=True))
        onehot = (sub == lab[:, nodes]).astype(F32)
        weight = msk[:, nodes].astype(F32)
        loss = loss + weight * (log_norm - jnp.sum(logits * onehot, axis=0, keepdims=True))
        prob = jnp.where(sub < CLS, jnp.exp(logits - log_norm), 0.0)
        lgrad_s[j, 0:CLS_ROWS] = ((weight / counted) * (prob - onehot)).astype(BF16)
        back = jnp.dot(wpad_t[...], lgrad_s[j], preferred_element_type=F32)
        grad_pre = (back * sig * (1.0 + pre * (1.0 - sig))).astype(BF16)
        pre_s[j] = grad_pre
        feed = jnp.dot(win[...], grad_pre, preferred_element_type=F32).astype(BF16)
        for c in (0, 1):
            for u in (0, 1):
                gt[c][col * OWN + 2 * j + u] = feed[c * WIDE : (c + 1) * WIDE, u * TILE : (u + 1) * TILE]
    loss = jnp.sum(loss, axis=1, keepdims=True) / counted

    steps = {}

    def weight_grads():
        gin_s[...] = jnp.zeros((TILE, HID), F32)
        gout_s[...] = jnp.zeros((HID, HID), F32)

        @pl.loop(0, OWN // 2)
        def _(j):
            gin_s[...] += lax.dot_general(rows_s[j], pre_s[j], NT, preferred_element_type=F32)
            gout_s[...] += lax.dot_general(lgrad_s[j], hid_s[j], NT, preferred_element_type=F32)

        sub = lax.broadcasted_iota(I32, (8, HID), 0)
        lane = lax.broadcasted_iota(I32, (8, HID), 1)
        tail = gout_s[HID - 8 : HID]
        gout_s[HID - 8 : HID] = jnp.where((sub == 7) & (lane == 0), jnp.broadcast_to(loss, (8, HID)), tail)
        for n in range(16):
            for r in range(0, 24, 8):
                at = n * 24 + r
                piece = gin_s[at : at + 8] if at < TILE else gout_s[at - TILE : at - TILE + 8]
                m_part[n // 4, n % 4, r : r + 8] = piece
        steps["y"] = [copy(m_part.at[(y + d) % 4], y_in.at[d - 1], to) for d, to in zip((1, 2, 3), y_others)]

    def sum_y():
        for c in steps["y"]:
            c.wait_recv()
        for n in range(4):
            m_y[n] = m_part[y, n] + y_in[0, n] + y_in[1, n] + y_in[2, n]
        steps["x"] = [copy(m_y.at[(x + d) % 4], x_in.at[d - 1], to) for d, to in zip((1, 2, 3), x_others)]

    def sum_x():
        for c in steps["x"]:
            c.wait_recv()
        me = zh * 2 + zl
        z_all[me] = m_y[x] + x_in[0] + x_in[1] + x_in[2]
        steps["z"] = [copy(z_all.at[me], z_all.at[me], to) for to in z_others]

    def sum_z():
        for c in steps["z"]:
            c.wait_recv()
        c_out[...] = (z_all[0] + z_all[1]) + (z_all[2] + z_all[3])
        steps["core"] = [copy(c_out, c_in, core)]

    def sum_core():
        for c in steps["core"]:
            c.wait_recv()
        final[x, y] = c_out[...] + c_in[...]
        steps["spread_y"] = [copy(final.at[x, y], final.at[x, y], to) for to in y_others]

    def spread_x():
        for c in steps["spread_y"]:
            c.wait_recv()
        steps["spread_x"] = [copy(final.at[x], final.at[x], to) for to in x_others]

    handed = ([], [])

    def hand(chunk):
        def landed(dr, dp, half):
            at = gt[chunk].at[pl.ds((col_chip(dr, dp) * 2 + k) * OWN + half * HALF, HALF)]
            handed[chunk].append(copy(at, at, core))

        return landed

    def take_hand(chunk):
        for c in handed[chunk]:
            c.wait_recv()

    def take_grads(chunk):
        def result(t, value):
            gf_t[t, chunk * WIDE : chunk * WIDE + WIDE] = value

        return result

    def backward_source(chunk):
        def source(dr, dp):
            base = row_chip(dr, dp) * OWN
            return lambda t: col_sum(chunk, base + t)

        return source

    gather_a, gather_b = (
        gather(copy, gt[c], lambda dr, dp: col_chip(dr, dp) * 2 + k, x_at, x_pair, hand(c)) for c in (0, 1)
    )
    scatter_a, scatter_b = (
        scatter(copy, out4, in4, c, y_at, y_pair, backward_source(c), take_grads(c)) for c in (0, 1)
    )
    run_to(gather_a, "own")
    for half in (0, 1):
        hand(0)(0, 0, half)
    run_to(gather_a, "left")
    run_to(gather_b, "own")
    for half in (0, 1):
        hand(1)(0, 0, half)
    weight_grads()
    run_to(gather_a, "beside")
    run_to(gather_b, "far")
    run_to(gather_a, "last")
    run_to(gather_b, "beside")
    run_to(gather_b, "last")
    sum_y()
    run_to(gather_a, "done")
    take_hand(0)
    backward(0)
    run_to(scatter_a, "start")
    sum_x()
    run_to(gather_b, "done")
    take_hand(1)
    backward(1)
    run_to(scatter_b, "start")
    run_to(scatter_a, "far")
    run_to(scatter_a, "near")
    sum_z()
    run_to(scatter_b, "far")
    sum_core()
    run_to(scatter_a, "late")
    run_to(scatter_b, "near")
    spread_x()
    run_to(scatter_b, "late")
    run_to(scatter_a, "done")
    run_to(scatter_b, "done")
    for t in range(OWN):
        gf_o[t] = gf_t[t].T

    for c in steps["spread_x"]:
        c.wait_recv()
    for n in range(16):
        for r in range(0, 24, 8):
            at = n * 24 + r
            piece = final[n % 4, n // 4, r : r + 8]
            if at < TILE:
                gin_o[at : at + 8] = piece
            else:
                put = min(8, CLS - (at - TILE))
                if put > 0:
                    gout_o[at - TILE : at - TILE + put] = piece[0:put]
                if at == TILE + HID - 8:
                    loss_o[...] = jnp.broadcast_to(piece[7:8, 0:1], loss_o.shape)

    for c in copies:
        c.wait_send()


def hand_out(loss, gin, gout, gf, loss_o, gin_o, gout_o, gf_o):
    loss_o[0] = loss[0, 0]
    gin_o[...] = gin[...]
    gout_o[...] = gout[...]
    gf_o[...] = gf[...]


def shards(
    features,
    tile_values,
    tile_rows,
    tile_cols,
    tile_counts,
    in_weight,
    out_weight,
    labels,
    loss_mask,
):
    vmem = pl.BlockSpec(memory_space=pltpu.VMEM)
    smem = pl.BlockSpec(memory_space=pltpu.SMEM)
    hbm = pl.BlockSpec(memory_space=pl.ANY)
    block = (OWN, TILE, TILE)
    loss, grad_in, grad_out, grad_features = pl.pallas_call(
        kernel,
        out_shape=(
            pltpu.VMEM((8, TILE), F32),
            pltpu.VMEM((TILE, HID), F32),
            pltpu.VMEM((CLS, HID), F32),
            pltpu.VMEM(block, F32),
        ),
        in_specs=[hbm] * 9,
        out_specs=(vmem, vmem, vmem, vmem),
        scratch_shapes=[
            pltpu.VMEM((1, SLOTS), I32),
            pltpu.VMEM((1, SLOTS), I32),
            pltpu.VMEM((1, 1), I32),
            pltpu.VMEM((TILE, HID), BF16),
            pltpu.VMEM((CLS, HID), BF16),
            pltpu.VMEM((1, OWN * TILE), I32),
            pltpu.VMEM((1, OWN * TILE), I32),
            pltpu.VMEM(block, BF16),
            pltpu.VMEM((SLOTS, TILE, TILE), BF16),
            pltpu.VMEM((SLOTS, TILE, TILE), BF16),
            *(pltpu.VMEM((COL_TILES, WIDE, TILE), BF16) for _ in range(2)),
            *(pltpu.VMEM((ROW_TILES, WIDE, TILE), BF16) for _ in range(2)),
            pltpu.VMEM((2, SLOTS, WIDE, TILE), F32),
            pltpu.VMEM((2, 8, OWN, WIDE, TILE), F32),
            pltpu.VMEM((2, 8, OWN, WIDE, TILE), F32),
            pltpu.VMEM(block, F32),
            pltpu.VMEM((16, TILE), I32),
            pltpu.SMEM((16, TILE), I32),
            pltpu.VMEM((HID, TILE), BF16),
            pltpu.VMEM((HID, HID), BF16),
            pltpu.VMEM((HID, HID), BF16),
            pltpu.VMEM((OWN // 2, TILE, 2 * TILE), BF16),
            pltpu.VMEM((OWN // 2, HID, 2 * TILE), BF16),
            pltpu.VMEM((OWN // 2, HID, 2 * TILE), BF16),
            pltpu.VMEM((OWN // 2, HID, 2 * TILE), BF16),
            pltpu.VMEM((TILE, HID), F32),
            pltpu.VMEM((HID, HID), F32),
            pltpu.VMEM((4, 4, 24, HID), F32),
            pltpu.VMEM((3, 4, 24, HID), F32),
            pltpu.VMEM((4, 24, HID), F32),
            pltpu.VMEM((3, 24, HID), F32),
            pltpu.VMEM((4, 24, HID), F32),
            pltpu.VMEM((24, HID), F32),
            pltpu.VMEM((24, HID), F32),
            pltpu.VMEM((4, 4, 24, HID), F32),
            pltpu.VMEM((5, 8, TILE), F32),
            pltpu.VMEM((4, 3, 8, TILE), F32),
            pltpu.SemaphoreType.DMA((N_SEMS,)),
            pltpu.SemaphoreType.DMA((N_SEMS,)),
            pltpu.SemaphoreType.DMA((10,)),
            *(pltpu.VMEM((2, OWN, WIDE, TILE), wire) for kinds in (WIRE2, WIRE2, WIRE4, WIRE4) for wire in kinds),
        ],
        compiler_params=pltpu.CompilerParams(
            collective_id=0, has_side_effects=True, vmem_limit_bytes=56 * 1024 * 1024
        ),
        name="graph_layer",
    )(
        features.reshape(OWN, TILE, TILE),
        tile_values,
        tile_rows[0],
        tile_cols[0],
        tile_counts,
        in_weight,
        out_weight.T,
        labels,
        loss_mask,
    )
    shapes = [pltpu.with_memory_space_constraint(v, pltpu.VMEM) for v in (loss, grad_in, grad_out, grad_features)]
    loss, grad_in, grad_out, grad_features = pl.pallas_call(
        hand_out,
        out_shape=(jax.ShapeDtypeStruct((1,), F32), *(jax.ShapeDtypeStruct(s.shape, F32) for s in shapes[1:])),
        in_specs=[vmem] * 4,
        out_specs=(smem, vmem, vmem, vmem),
        name="hand_out",
    )(*shapes)
    return loss.reshape(()), grad_in, grad_out.T, grad_features.reshape(1, OWN * TILE, TILE)


def solution(mesh):
    placed = (
        P("col", "row", None),
        P("row", "col", None, None, None),
        P("row", "col", None),
        P("row", "col", None),
        P("row", "col"),
        P(),
        P(),
        P("row", "col"),
        P("row", "col"),
    )
    return jax.shard_map(
        shards,
        mesh=mesh,
        in_specs=placed,
        out_specs=(P(), P(), P(), P("col", "row", None)),
        check_vma=False,
    )
```

time: 381 us -> 80.4 us (0.21)
  blocking collectives: 179 us -> 0 us
  Pallas kernels: 0 us -> 78.8 us
  waiting for transfers between devices: 61.2 us -> 0 us
  matrix products: 46.6 us -> 0 us
  other arithmetic: 43.9 us -> 0 us
  local copies, waits for them, and re-layouts: 33.3 us -> 0 us
  between operations: 15.8 us -> 1.29 us
    psum x3 -> x0, blocking collectives: 134 us -> none  [the longest x1 97.7 us: shards(): summed = lax.psum(partial_value, 'col')]
    pallas_call x0 -> x2, Pallas kernels: none -> 78.8 us  [the longest x1 77.9 us: shards(): pl.pallas_call(kernel, out_shape=(pltpu.VMEM((8, TILE), F32), pltpu.VMEM(...]
    reduce_scatter x1 -> x0, waiting for transfers between devices: 48.4 us -> none  [shards(): lax.psum_scatter(column_part, 'row', scatter_dimension=0, tiled=True)]
    dot_general x8 -> x0, matrix products: 46.6 us -> none  [the longest x1 11.5 us: dense_head(): lax.dot_general(log_grad, out_weight, (((1,), (1,)), ((), ())), preferred...]
    all_gather x2 -> x0, blocking collectives: 45 us -> none  [the longest x1 25.6 us: shards(): lax.all_gather(loss_mask, 'col', axis=1, tiled=True)]
    scatter-add x2 -> x0, other arithmetic: 40.1 us -> none  [the longest x1 20.2 us: shards(): jax.ops.segment_sum(product, tile_rows[0, 0], num_segments=row_tiles)]
    mul x2 -> x0, local copies, waits for them, and re-layouts: 13.2 us -> none  [the longest x1 6.62 us: shards(): jnp.einsum('tab,taf->tbf', values, grad_tiles, preferred_element_type=jnp...]
    psum x1 -> x0, waiting for transfers between devices: 12.1 us -> none  [shards(): lax.psum((loss_part, grad_in, grad_out), 'row')]
  transfers between devices with their start and end apart: 3 -> 0, of which waited for: 2 -> 0; matrix products, arithmetic and copies ran while one was open for 11% -> 0% of each run, Pallas kernels for 0% -> 0%
where the time goes in v2:
time: 80.4 us; the launch traced here: 80.1 us
  Pallas kernels  78.8 us (98%)
  between operations  1.29 us (2%)
    pallas_call x1, Pallas kernels, shards(): pl.pallas_call(kernel, out_shape=(pltpu.VMEM((8, TILE), F32), pltpu.VMEM(...  77.9 us

profile of v2, /device:TPU:0, one launch (start us, length us, event | category | flops | bytes accessed | tf_op | source)
XLA Modules:
  0.0 80.1 jit_solution(649156250934330944)
XLA Ops:
  1.3 77.9 %graph_layer.1 = (f32[8,128]{1,0:T(8,128)S(1)}, f32[128,256]{1,0:T(8,128)S(1)}, f32[172,256]{1,0:T(8,128)S(1)}, f32[6,128,128]{2,1,0:T(8,128)S(1)}) custom-call(bf16[6,128,128]{2,1,0:T(8,128)(2,1)} %bitcast.7, bf16[1,1,96,128,128]{4,3,2,1,0:T(8,128)(2,1)} %vals_hbm.1, s32[1,96]{1,0:T(1,128)} %bitcast.9, s32[1,96]{1,0:T(1,128)} %bitcast.10, ...), custom_call_target="tpu_custom_call" | custom-call | tf_op jit(solution)/shard_map/graph_layer/pallas_call | solution.py:580
  79.2 0.9 %hand_out.1 = (f32[1]{0:T(128)}, f32[128,256]{1,0:T(8,128)}, f32[172,256]{1,0:T(8,128)}, f32[6,128,128]{2,1,0:T(8,128)}) custom-call(f32[8,128]{1,0:T(8,128)S(1)} %get-tuple-element.12.loss, f32[128,256]{1,0:T(8,128)S(1)} %get-tuple-element.13.gin, f32[172,256]{1,0:T(8,128)S(1)} %get-tuple-element.14.gout, f32[6,128,128]{2,1,0:T(8,128)S(1)} %get-tuple-element.15.gf), custom_call_target="tpu_custom_call" | custom-call | tf_op jit(solution)/shard_map/hand_out/pallas_call | solution.py:649

commit v3 on v2

v3 whole, which is shorter than its diff:
```python
import jax
import jax.numpy as jnp
from jax import lax
from jax.experimental import pallas as pl
from jax.experimental.pallas import tpu as pltpu
from jax.sharding import PartitionSpec as P

F32, BF16, I32 = jnp.float32, jnp.bfloat16, jnp.int32
TILE = 128
CHUNKS = ((0, 64), (64, 64))
SLOTS = 96
ROW_TILES = 96
COL_TILES = 48
OWN = 6
HALF = 3
CLS = 172
CLS_ROWS = 176
HID = 256
UNROLL = 48
N_SEMS = 86
WIDER2 = (True, True)
WIDER4 = (True, True)
FAR_PAIR, SIDE_UP, SIDE_DOWN, FREE, FAR, LATE, NEAR = range(7)
FORWARD = (
    ("gather", 0, "own"), ("gather", 1, "own"), ("gather", 0, "far"), ("slots", 0, ""),
    ("weights", 0, ""), ("gather", 1, "far"), ("gather", 0, "beside"), ("turn", 0, ""),
    ("gather", 0, "last"), ("count", 0, ""), ("gather", 1, "beside"), ("gather", 1, "last"),
    ("gather", 0, "done"), ("products", 0, ""), ("count", 1, ""), ("cores", 0, ""),
    ("gather", 1, "done"), ("products", 1, ""), ("scatter", 0, "start"), ("cores", 1, ""),
    ("scatter", 1, "start"), ("count", 2, ""), ("scatter", 0, "far"), ("scatter", 0, "near"),
    ("count", 3, ""), ("scatter", 1, "far"), ("scatter", 1, "near"), ("scatter", 0, "late"),
    ("scatter", 1, "late"), ("scatter", 0, "done"), ("scatter", 1, "done"),
)
BACKWARD = (
    ("gather", 0, "own"), ("small", 0, ""), ("gather", 1, "own"), ("gather", 0, "far"),
    ("gather", 1, "far"), ("gather", 0, "beside"), ("gather", 0, "last"), ("small", 1, ""),
    ("gather", 1, "beside"), ("gather", 1, "last"), ("small", 2, ""), ("gather", 0, "done"),
    ("handed", 0, ""), ("products", 0, ""), ("scatter", 0, "start"), ("gather", 1, "done"),
    ("small", 3, ""), ("handed", 1, ""), ("products", 1, ""), ("small", 4, ""),
    ("scatter", 0, "far"), ("scatter", 1, "start"), ("scatter", 0, "near"), ("scatter", 1, "far"),
    ("small", 5, ""), ("scatter", 1, "near"), ("scatter", 0, "late"), ("scatter", 1, "late"),
    ("scatter", 0, "done"), ("scatter", 1, "done"),
)
NT = (((1,), (1,)), ((), ()))


def gather(copy, counter, buf, block, ring, pair, landed):
    def expect(blocks):
        return counter(buf.at[0 : blocks * OWN])

    def send(dr, dp, half, to, recv):
        at = buf.at[pl.ds(block(dr, dp) * OWN + half * HALF, HALF)]
        copy(at, at, to, sent, recv)

    up, down, across = ring(1), ring(-1), pair
    sent, first, beside, far, rest = expect(7), expect(1), expect(1), expect(1), expect(4)
    send(0, 0, 0, up, first)
    send(0, 0, 1, down, first)
    send(0, 0, 0, across, beside)
    send(0, 0, 1, up, rest)
    send(0, 0, 0, down, rest)
    send(0, 0, 1, across, beside)
    yield "own"
    first.wait()
    send(-1, 0, 0, up, far)
    send(1, 0, 1, down, far)
    landed(-1, 0, 0)
    landed(1, 0, 1)
    yield "far"
    beside.wait()
    for half in (0, 1):
        send(0, 1, half, up, rest)
        send(0, 1, half, down, rest)
    landed(0, 1)
    yield "beside"
    far.wait()
    send(2, 0, 0, across, rest)
    send(2, 0, 1, across, rest)
    landed(2, 0)
    yield "last"
    rest.wait()
    landed(-1, 0, 1)
    landed(1, 0, 0)
    landed(-1, 1)
    landed(1, 1)
    landed(2, 1)
    yield "done"


def scatter(copy, counter, out, inn, out_near, in_near, ring, pair, source, result):
    up, down, across = ring(1), ring(-1), pair
    both = (0, OWN)
    low, high = (0, HALF), (HALF, OWN)

    def fill(ref, span, chip, *received):
        local = source(*chip)
        for t in range(*span):
            value = local(t)
            for n in received:
                value = value + inn[n, t].astype(F32)
            ref[t] = value.astype(ref.dtype)

    def send(slot, span, to, recv):
        at = pl.ds(span[0], span[1] - span[0])
        copy(out.at[slot, at], inn.at[slot, at], to, sent, recv)

    sent, sent_near = counter(out.at[0:NEAR]), counter(out_near)
    far_pair = [counter(inn.at[FAR_PAIR, a:b]) for a, b in (low, high)]
    side, free, far, late = counter(inn.at[0:2]), counter(inn.at[0]), counter(inn.at[0]), counter(inn.at[0])
    near = counter(in_near)
    for n, span in enumerate((low, high)):
        fill(out.at[FAR_PAIR], span, (2, 1))
        send(FAR_PAIR, span, across, far_pair[n])
    fill(out.at[SIDE_UP], both, (1, 1))
    send(SIDE_UP, both, up, side)
    fill(out.at[SIDE_DOWN], both, (-1, 1))
    send(SIDE_DOWN, both, down, side)
    fill(out.at[FREE], high, (1, 0))
    send(FREE, high, up, free)
    fill(out.at[FREE], low, (-1, 0))
    send(FREE, low, down, free)
    yield "start"
    far_pair[0].wait()
    fill(out.at[FAR], low, (2, 0), FAR_PAIR)
    send(FAR, low, up, far)
    far_pair[1].wait()
    fill(out.at[FAR], high, (2, 0), FAR_PAIR)
    send(FAR, high, down, far)
    yield "far"
    side.wait()
    for a, b in (low, high):
        fill(out_near, (a, b), (0, 1), SIDE_UP, SIDE_DOWN)
        copy(out_near.at[a:b], in_near.at[a:b], across, sent_near, near)
    yield "near"
    far.wait()
    fill(out.at[LATE], low, (1, 0), FAR)
    send(LATE, low, up, late)
    fill(out.at[LATE], high, (-1, 0), FAR)
    send(LATE, high, down, late)
    yield "late"
    free.wait()
    near.wait()
    late.wait()
    local = source(0, 0)
    for t in range(OWN):
        value = local(t) + inn[FREE, t].astype(F32) + inn[LATE, t].astype(F32)
        result(t, value + in_near[t].astype(F32))
    yield "done"


def order_slots(key, other, live, slots, tiles, idx, base):
    sub = lax.broadcasted_iota(I32, (slots, slots), 0)
    lane = lax.broadcasted_iota(I32, (slots, slots), 1)
    diag = sub == lane

    def column(v):
        return jnp.sum(jnp.where(diag, jnp.broadcast_to(v, (slots, slots)), 0), axis=1, keepdims=True)

    lane1 = lax.broadcasted_iota(I32, (1, slots), 1)
    sort_l = jnp.where(live > 0, key * TILE + lane1, tiles * TILE + lane1)
    sort_c, key_c, other_c, live_c = column(sort_l), column(key), column(other), column(live)
    rank_c = jnp.sum((jnp.broadcast_to(sort_l, (slots, slots)) < sort_c).astype(I32), axis=1, keepdims=True)

    def place(v):
        return jnp.sum(jnp.where(rank_c == lane, v, 0), axis=0, keepdims=True)

    idx[base : base + 1, 0:slots] = place(sub)
    idx[base + 1 : base + 2, 0:slots] = place(other_c)
    idx[base + 2 : base + 3, 0:slots] = place(key_c)
    below = jnp.sum(jnp.where(key_c <= lane, live_c, 0), axis=0, keepdims=True)
    same = jnp.sum(jnp.where(key_c == lane, live_c, 0), axis=0, keepdims=True)
    idx[base + 3 : base + 4, 0:slots] = jnp.maximum(below - 1, 0)
    idx[base + 4 : base + 5, 0:slots] = same


def tile_products(product, sums, where, base):
    def step(i, acc):
        for u in range(UNROLL):
            k = i * UNROLL + u
            prod = product(where[base, k], where[base + 1, k])
            keep = where[base + 2, k] == where[base + 2, jnp.maximum(k - 1, 0)]
            acc = jnp.where(keep, acc, 0.0) + prod
            sums[k] = acc
        return acc

    lax.fori_loop(0, SLOTS // UNROLL, step, jnp.zeros(sums.shape[1:], F32))


class Counter:
    def __init__(self, sem, like):
        self.sem, self.like = sem, like
        self.waiting = True

    def wait(self):
        if self.waiting:
            self.waiting = False
            pltpu.make_async_copy(self.like, self.like, self.sem).wait()


def run_to(phase, step):
    while next(phase) != step:
        pass


def kernel(
    feat, vals_hbm, trow_h, tcol_h, tcnt_h, win_h, wout_h, lab_h, msk_h,
    loss_o, gin_o, gout_o, gf_o,
    trow, tcol, tcnt, win, wout, lab, msk,
    feat_v, vals, vals_t, gf_t,
    idx, where, win_t, wpad, wpad_t, rows_s, hid_s, lgrad_s, pre_s, gin_s, gout_s,
    m_part, y_in, m_y, x_in, z_all, c_out, c_in, final,
    cnt_out, cnt_in, sems, local_sem, *parts,
):
    row, col = lax.axis_index("row"), lax.axis_index("col")
    zl, y = row // 4, row % 4
    zh, x, k = col // 8, (col // 2) % 4, col % 2
    count = len(CHUNKS)
    xt, gt, sums, core_out, core_in = (parts[n * count : (n + 1) * count] for n in range(5))
    out2, in2, out4, in4, near_out2, near_in2, near_out4, near_in4 = (
        parts[n * count : (n + 1) * count] for n in range(5, 13)
    )

    def chip(zl_=zl, y_=y, zh_=zh, x_=x, k_=k):
        return {"row": zl_ * 4 + y_, "col": (zh_ * 4 + x_) * 2 + k_}

    def y_at(d):
        return chip(y_=(y + d + 4) % 4)

    def x_at(d):
        return chip(x_=(x + d + 4) % 4)

    def row_chip(dr, dp):
        return (zl + dp) % 2 * 4 + (y + dr + 4) % 4

    def col_chip(dr, dp):
        return (zh + dp) % 2 * 4 + (x + dr + 4) % 4

    z_others = [chip(zl_=1 - zl), chip(zh_=1 - zh), chip(zl_=1 - zl, zh_=1 - zh)]
    y_others = [y_at(d) for d in (1, 2, 3)]
    x_others = [x_at(d) for d in (1, 2, 3)]
    y_pair, x_pair, core = chip(zl_=1 - zl), chip(zh_=1 - zh), chip(k_=1 - k)

    counters = []

    def counter(like):
        counters.append(Counter(sems.at[len(counters)], like))
        return counters[-1]

    def copy(src, dst, to, send, recv):
        pltpu.make_async_remote_copy(
            src_ref=src, dst_ref=dst, send_sem=send.sem, recv_sem=recv.sem,
            device_id=to, device_id_type=pl.DeviceIdType.MESH,
        ).start()

    load_own = pltpu.make_async_copy(feat, feat_v, local_sem.at[0])
    load_own.start()
    load_vals = pltpu.make_async_copy(vals_hbm.at[0, 0], vals, local_sem.at[1])
    load_vals.start()
    pairs = ((trow_h, trow), (tcol_h, tcol), (tcnt_h, tcnt), (win_h, win), (wout_h, wout), (lab_h, lab), (msk_h, msk))
    loads = [pltpu.make_async_copy(src, dst, local_sem.at[3 + n]) for n, (src, dst) in enumerate(pairs)]
    for c in loads:
        c.start()

    partners = [*y_others, *x_others, *z_others, core]
    barrier = pltpu.get_barrier_semaphore()
    for p in partners:
        pl.semaphore_signal(barrier, inc=1, device_id=p, device_id_type=pl.DeviceIdType.MESH)
    load_own.wait()
    for t in range(OWN):
        turned = feat_v[t].astype(F32).T.astype(BF16)
        for c, (first, width) in enumerate(CHUNKS):
            xt[c][row * OWN + t] = turned[first : first + width]
    pl.semaphore_wait(barrier, len(partners))

    count_groups = [y_others, x_others, z_others, [core]]
    count_copies = []

    def count_send(stage):
        group = count_groups[stage]
        like = cnt_in.at[stage, 0 : len(group)]
        send, recv = counter(like), counter(like)
        for n, to in enumerate(group):
            copy(cnt_out.at[stage], cnt_in.at[stage, n], to, send, recv)
        count_copies.append(recv)

    def count_take(stage):
        count_copies[stage].wait()
        value = cnt_out[stage]
        for n in range(len(count_groups[stage])):
            value = value + cnt_in[stage, n]
        cnt_out[stage + 1] = value

    def prepare_slots():
        slot = lax.broadcasted_iota(I32, (1, SLOTS), 1)
        live = (slot < tcnt[...]).astype(I32)
        idx[...] = jnp.zeros(idx.shape, I32)
        order_slots(trow[...], tcol[...], live, SLOTS, ROW_TILES, idx, 0)
        order_slots(tcol[...], trow[...], live, SLOTS, ROW_TILES, idx, 5)
        to_smem = pltpu.make_async_copy(idx, where, local_sem.at[2])
        to_smem.start()
        to_smem.wait()

    def prepare_weights():
        win_t[...] = win[...].astype(F32).T.astype(BF16)
        wpad[...] = jnp.zeros(wpad.shape, BF16)
        wpad[0:CLS] = wout[...]
        wpad_t[...] = wpad[...].astype(F32).T.astype(BF16)
        lgrad_s[...] = jnp.zeros(lgrad_s.shape, BF16)

    def row_sum(chunk, tile):
        return sums[chunk][where[3, tile]] * (where[4, tile] > 0).astype(F32)

    def col_sum(chunk, tile):
        return sums[chunk][where[8, tile]] * (where[9, tile] > 0).astype(F32)

    def forward(chunk):
        def product(slot, other):
            return jnp.dot(xt[chunk][other], vals_t[slot], preferred_element_type=F32)

        tile_products(product, sums[chunk], where, 0)

    def backward(chunk):
        def product(slot, other):
            return jnp.dot(gt[chunk][other], vals[slot], preferred_element_type=F32)

        tile_products(product, sums[chunk], where, 5)

    classes = [(2, 1), (1, 1), (-1, 1), (1, 0), (-1, 0), (2, 0), (0, 1), (0, 0)]
    core_first, core_rest = {}, {}

    def core_send(chunk):
        send = counter(core_out[chunk])
        core_first[chunk], core_rest[chunk] = counter(core_in[chunk].at[0]), counter(core_in[chunk].at[1:8])
        for n, (dr, dp) in enumerate(classes):
            base = (col_chip(dr, dp) * 2 + 1 - k) * OWN
            for t in range(OWN):
                core_out[chunk][n, t] = row_sum(chunk, base + t)
            recv = core_rest[chunk] if n else core_first[chunk]
            copy(core_out[chunk].at[n], core_in[chunk].at[n], core, send, recv)

    def forward_source(chunk):
        def source(dr, dp):
            base, n = (col_chip(dr, dp) * 2 + k) * OWN, classes.index((dr, dp))
            (core_rest if n else core_first)[chunk].wait()
            return lambda t: row_sum(chunk, base + t) + core_in[chunk][n, t]

        return source

    def take_rows(chunk):
        first, width = CHUNKS[chunk]

        def result(t, value):
            lanes = slice(t % 2 * TILE, t % 2 * TILE + TILE)
            rows_s[t // 2, first : first + width, lanes] = value.astype(BF16)

        return result

    def turn_tiles():
        load_vals.wait()

        @pl.loop(0, SLOTS, unroll=8)
        def _(n):
            vals_t[n] = vals[n].T

    def count_step(stage):
        if stage == 0:
            cnt_out[0] = jnp.broadcast_to(jnp.sum(msk[...].astype(F32), axis=1, keepdims=True), (8, TILE))
        else:
            count_take(stage - 1)
        count_send(stage)

    gathers = [gather(copy, counter, xt[c], row_chip, y_at, y_pair, lambda *chip: None) for c in range(count)]
    scatters = [
        scatter(copy, counter, out2[c], in2[c], near_out2[c], near_in2[c], x_at, x_pair, forward_source(c), take_rows(c)) for c in range(count)
    ]
    loaded = False
    for what, c, step in FORWARD:
        if what in ("count", "slots", "weights") and not loaded:
            loaded = True
            for load in loads:
                load.wait()
        if what == "gather":
            run_to(gathers[c], step)
        elif what == "scatter":
            run_to(scatters[c], step)
        elif what == "products":
            forward(c)
        elif what == "cores":
            core_send(c)
        elif what == "count":
            count_step(c)
        elif what == "slots":
            prepare_slots()
        elif what == "weights":
            prepare_weights()
        elif what == "turn":
            turn_tiles()
    count_take(3)

    counted = cnt_out[4][0:1, 0:1]
    sub = lax.broadcasted_iota(I32, (CLS_ROWS, 2 * TILE), 0)
    loss = jnp.zeros((1, 2 * TILE), F32)
    for j in range(OWN // 2):
        nodes = slice(j * 2 * TILE, (j + 1) * 2 * TILE)
        pre = jnp.dot(win_t[...], rows_s[j], preferred_element_type=F32)
        sig = jax.nn.sigmoid(pre)
        hidden = (pre * sig).astype(BF16)
        hid_s[j] = hidden
        logits = jnp.dot(wpad[0:CLS_ROWS], hidden, preferred_element_type=F32)
        log_norm = jnp.log(jnp.sum(jnp.where(sub < CLS, jnp.exp(logits), 0.0), axis=0, keepdims=True))
        onehot = (sub == lab[:, nodes]).astype(F32)
        weight = msk[:, nodes].astype(F32)
        loss = loss + weight * (log_norm - jnp.sum(logits * onehot, axis=0, keepdims=True))
        prob = jnp.where(sub < CLS, jnp.exp(logits - log_norm), 0.0)
        lgrad_s[j, 0:CLS_ROWS] = ((weight / counted) * (prob - onehot)).astype(BF16)
        back = jnp.dot(wpad_t[...], lgrad_s[j], preferred_element_type=F32)
        grad_pre = (back * sig * (1.0 + pre * (1.0 - sig))).astype(BF16)
        pre_s[j] = grad_pre
        feed = jnp.dot(win[...], grad_pre, preferred_element_type=F32).astype(BF16)
        for c, (first, width) in enumerate(CHUNKS):
            for u in (0, 1):
                gt[c][col * OWN + 2 * j + u] = feed[first : first + width, u * TILE : (u + 1) * TILE]
    loss = jnp.sum(loss, axis=1, keepdims=True) / counted

    steps = {}

    def spread(name, like, moves):
        send, steps[name] = counter(like), counter(like)
        for src, dst, to in moves:
            copy(src, dst, to, send, steps[name])

    def weight_grads():
        gin_s[...] = jnp.zeros((TILE, HID), F32)
        gout_s[...] = jnp.zeros((HID, HID), F32)

        @pl.loop(0, OWN // 2)
        def _(j):
            gin_s[...] += lax.dot_general(rows_s[j], pre_s[j], NT, preferred_element_type=F32)
            gout_s[...] += lax.dot_general(lgrad_s[j], hid_s[j], NT, preferred_element_type=F32)

        sub = lax.broadcasted_iota(I32, (8, HID), 0)
        lane = lax.broadcasted_iota(I32, (8, HID), 1)
        tail = gout_s[HID - 8 : HID]
        gout_s[HID - 8 : HID] = jnp.where((sub == 7) & (lane == 0), jnp.broadcast_to(loss, (8, HID)), tail)
        for n in range(16):
            for r in range(0, 24, 8):
                at = n * 24 + r
                piece = gin_s[at : at + 8] if at < TILE else gout_s[at - TILE : at - TILE + 8]
                m_part[n // 4, n % 4, r : r + 8] = piece
        spread("y", y_in, [(m_part.at[(y + d) % 4], y_in.at[d - 1], to) for d, to in zip((1, 2, 3), y_others)])

    def sum_y():
        steps["y"].wait()
        for n in range(4):
            m_y[n] = m_part[y, n] + y_in[0, n] + y_in[1, n] + y_in[2, n]
        spread("x", x_in, [(m_y.at[(x + d) % 4], x_in.at[d - 1], to) for d, to in zip((1, 2, 3), x_others)])

    def sum_x():
        steps["x"].wait()
        me = zh * 2 + zl
        z_all[me] = m_y[x] + x_in[0] + x_in[1] + x_in[2]
        spread("z", z_all.at[0:3], [(z_all.at[me], z_all.at[me], to) for to in z_others])

    def sum_z():
        steps["z"].wait()
        c_out[...] = (z_all[0] + z_all[1]) + (z_all[2] + z_all[3])
        spread("core", c_in, [(c_out, c_in, core)])

    def sum_core():
        steps["core"].wait()
        final[x, y] = c_out[...] + c_in[...]
        spread("spread_y", final.at[0, 0:3], [(final.at[x, y], final.at[x, y], to) for to in y_others])

    def spread_x():
        steps["spread_y"].wait()
        spread("spread_x", final.at[0:3], [(final.at[x], final.at[x], to) for to in x_others])

    handed = [(counter(gt[c].at[0 : 8 * OWN]), counter(gt[c].at[0 : 8 * OWN])) for c in range(count)]

    def hand(chunk):
        def landed(dr, dp, half=None):
            first, size = (0, OWN) if half is None else (half * HALF, HALF)
            at = gt[chunk].at[pl.ds((col_chip(dr, dp) * 2 + k) * OWN + first, size)]
            copy(at, at, core, *handed[chunk])

        return landed

    def take_grads(chunk):
        first, width = CHUNKS[chunk]

        def result(t, value):
            gf_t[t, first : first + width] = value

        return result

    def backward_source(chunk):
        def source(dr, dp):
            base = row_chip(dr, dp) * OWN
            return lambda t: col_sum(chunk, base + t)

        return source

    gathers = [
        gather(copy, counter, gt[c], lambda dr, dp: col_chip(dr, dp) * 2 + k, x_at, x_pair, hand(c)) for c in range(count)
    ]
    scatters = [
        scatter(copy, counter, out4[c], in4[c], near_out4[c], near_in4[c], y_at, y_pair, backward_source(c), take_grads(c)) for c in range(count)
    ]
    small = (weight_grads, sum_y, sum_x, sum_z, sum_core, spread_x)
    for what, c, step in BACKWARD:
        if what == "gather":
            run_to(gathers[c], step)
            if step == "own":
                hand(c)(0, 0)
        elif what == "scatter":
            run_to(scatters[c], step)
        elif what == "handed":
            handed[c][1].wait()
        elif what == "products":
            backward(c)
        elif what == "small":
            small[c]()
    for t in range(OWN):
        gf_o[t] = gf_t[t].T

    steps["spread_x"].wait()
    for n in range(16):
        for r in range(0, 24, 8):
            at = n * 24 + r
            piece = final[n % 4, n // 4, r : r + 8]
            if at < TILE:
                gin_o[at : at + 8] = piece
            else:
                put = min(8, CLS - (at - TILE))
                if put > 0:
                    gout_o[at - TILE : at - TILE + put] = piece[0:put]
                if at == TILE + HID - 8:
                    loss_o[...] = jnp.broadcast_to(piece[7:8, 0:1], loss_o.shape)

    for c in counters:
        c.wait()


def hand_out(loss, gin, gout, gf, loss_o, gin_o, gout_o, gf_o):
    loss_o[0] = loss[0, 0]
    gin_o[...] = gin[...]
    gout_o[...] = gout[...]
    gf_o[...] = gf[...]


def shards(
    features,
    tile_values,
    tile_rows,
    tile_cols,
    tile_counts,
    in_weight,
    out_weight,
    labels,
    loss_mask,
):
    vmem = pl.BlockSpec(memory_space=pltpu.VMEM)
    smem = pl.BlockSpec(memory_space=pltpu.SMEM)
    hbm = pl.BlockSpec(memory_space=pl.ANY)
    block = (OWN, TILE, TILE)
    loss, grad_in, grad_out, grad_features = pl.pallas_call(
        kernel,
        out_shape=(
            pltpu.VMEM((8, TILE), F32),
            pltpu.VMEM((TILE, HID), F32),
            pltpu.VMEM((CLS, HID), F32),
            pltpu.VMEM(block, F32),
        ),
        in_specs=[hbm] * 9,
        out_specs=(vmem, vmem, vmem, vmem),
        scratch_shapes=[
            pltpu.VMEM((1, SLOTS), I32),
            pltpu.VMEM((1, SLOTS), I32),
            pltpu.VMEM((1, 1), I32),
            pltpu.VMEM((TILE, HID), BF16),
            pltpu.VMEM((CLS, HID), BF16),
            pltpu.VMEM((1, OWN * TILE), I32),
            pltpu.VMEM((1, OWN * TILE), I32),
            pltpu.VMEM(block, BF16),
            pltpu.VMEM((SLOTS, TILE, TILE), BF16),
            pltpu.VMEM((SLOTS, TILE, TILE), BF16),
            pltpu.VMEM(block, F32),
            pltpu.VMEM((16, TILE), I32),
            pltpu.SMEM((16, TILE), I32),
            pltpu.VMEM((HID, TILE), BF16),
            pltpu.VMEM((HID, HID), BF16),
            pltpu.VMEM((HID, HID), BF16),
            pltpu.VMEM((OWN // 2, TILE, 2 * TILE), BF16),
            pltpu.VMEM((OWN // 2, HID, 2 * TILE), BF16),
            pltpu.VMEM((OWN // 2, HID, 2 * TILE), BF16),
            pltpu.VMEM((OWN // 2, HID, 2 * TILE), BF16),
            pltpu.VMEM((TILE, HID), F32),
            pltpu.VMEM((HID, HID), F32),
            pltpu.VMEM((4, 4, 24, HID), F32),
            pltpu.VMEM((3, 4, 24, HID), F32),
            pltpu.VMEM((4, 24, HID), F32),
            pltpu.VMEM((3, 24, HID), F32),
            pltpu.VMEM((4, 24, HID), F32),
            pltpu.VMEM((24, HID), F32),
            pltpu.VMEM((24, HID), F32),
            pltpu.VMEM((4, 4, 24, HID), F32),
            pltpu.VMEM((5, 8, TILE), F32),
            pltpu.VMEM((4, 3, 8, TILE), F32),
            pltpu.SemaphoreType.DMA((N_SEMS,)),
            pltpu.SemaphoreType.DMA((10,)),
            *(pltpu.VMEM((COL_TILES, width, TILE), BF16) for _, width in CHUNKS),
            *(pltpu.VMEM((ROW_TILES, width, TILE), BF16) for _, width in CHUNKS),
            *(pltpu.VMEM((SLOTS, width, TILE), F32) for _, width in CHUNKS),
            *(pltpu.VMEM((8, OWN, width, TILE), F32) for _, width in CHUNKS),
            *(pltpu.VMEM((8, OWN, width, TILE), F32) for _, width in CHUNKS),
            *(pltpu.VMEM((NEAR, OWN, width, TILE), BF16) for _ in range(4) for _, width in CHUNKS),
            *(
                pltpu.VMEM((OWN, width, TILE), F32 if wider[c] else BF16)
                for wider in (WIDER2, WIDER2, WIDER4, WIDER4)
                for c, (_, width) in enumerate(CHUNKS)
            ),
        ],
        compiler_params=pltpu.CompilerParams(
            collective_id=0, has_side_effects=True, vmem_limit_bytes=56 * 1024 * 1024
        ),
        name="graph_layer",
    )(
        features.reshape(OWN, TILE, TILE),
        tile_values,
        tile_rows[0],
        tile_cols[0],
        tile_counts,
        in_weight,
        out_weight.T,
        labels,
        loss_mask,
    )
    shapes = [pltpu.with_memory_space_constraint(v, pltpu.VMEM) for v in (loss, grad_in, grad_out, grad_features)]
    loss, grad_in, grad_out, grad_features = pl.pallas_call(
        hand_out,
        out_shape=(jax.ShapeDtypeStruct((1,), F32), *(jax.ShapeDtypeStruct(s.shape, F32) for s in shapes[1:])),
        in_specs=[vmem] * 4,
        out_specs=(smem, vmem, vmem, vmem),
        name="hand_out",
    )(*shapes)
    return loss.reshape(()), grad_in, grad_out.T, grad_features.reshape(1, OWN * TILE, TILE)


def solution(mesh):
    placed = (
        P("col", "row", None),
        P("row", "col", None, None, None),
        P("row", "col", None),
        P("row", "col", None),
        P("row", "col"),
        P(),
        P(),
        P("row", "col"),
        P("row", "col"),
    )
    return jax.shard_map(
        shards,
        mesh=mesh,
        in_specs=placed,
        out_specs=(P(), P(), P(), P("col", "row", None)),
        check_vma=False,
    )
```

time: 80.4 us -> 75.2 us (0.935)
  Pallas kernels: 78.8 us -> 73.8 us
    pallas_call x1, Pallas kernels: 77.9 us -> 72.9 us  [shards(): pl.pallas_call(kernel, out_shape=(pltpu.VMEM((8, TILE), F32), pltpu.VMEM(...]
where the time goes in v3:
time: 75.2 us; the launch traced here: 75.1 us
  Pallas kernels  73.8 us (98%)
  between operations  1.29 us (2%)
    pallas_call x1, Pallas kernels, shards(): pl.pallas_call(kernel, out_shape=(pltpu.VMEM((8, TILE), F32), pltpu.VMEM(...  72.9 us

profile of v3, /device:TPU:0, one launch (start us, length us, event | category | flops | bytes accessed | tf_op | source)
XLA Modules:
  0.0 75.1 jit_solution(1673102224026327460)
XLA Ops:
  1.3 72.9 %graph_layer.1 = (f32[8,128]{1,0:T(8,128)S(1)}, f32[128,256]{1,0:T(8,128)S(1)}, f32[172,256]{1,0:T(8,128)S(1)}, f32[6,128,128]{2,1,0:T(8,128)S(1)}) custom-call(bf16[6,128,128]{2,1,0:T(8,128)(2,1)} %bitcast.7, bf16[1,1,96,128,128]{4,3,2,1,0:T(8,128)(2,1)} %vals_hbm.1, s32[1,96]{1,0:T(1,128)} %bitcast.9, s32[1,96]{1,0:T(1,128)} %bitcast.10, ...), custom_call_target="tpu_custom_call" | custom-call | tf_op jit(solution)/shard_map/graph_layer/pallas_call | solution.py:566
  74.2 0.9 %hand_out.1 = (f32[1]{0:T(128)}, f32[128,256]{1,0:T(8,128)}, f32[172,256]{1,0:T(8,128)}, f32[6,128,128]{2,1,0:T(8,128)}) custom-call(f32[8,128]{1,0:T(8,128)S(1)} %get-tuple-element.12.loss, f32[128,256]{1,0:T(8,128)S(1)} %get-tuple-element.13.gin, f32[172,256]{1,0:T(8,128)S(1)} %get-tuple-element.14.gout, f32[6,128,128]{2,1,0:T(8,128)S(1)} %get-tuple-element.15.gf), custom_call_target="tpu_custom_call" | custom-call | tf_op jit(solution)/shard_map/hand_out/pallas_call | solution.py:639

commit v4 on v3

--- a/solution.py
+++ b/solution.py
@@ -18,7 +18,7 @@
 HID = 256
 UNROLL = 48
 N_SEMS = 86
-WIDER2 = (True, True)
+WIDER2 = (True, False)
 WIDER4 = (True, True)
 FAR_PAIR, SIDE_UP, SIDE_DOWN, FREE, FAR, LATE, NEAR = range(7)
 FORWARD = (
@@ -32,7 +32,7 @@
     ("scatter", 1, "late"), ("scatter", 0, "done"), ("scatter", 1, "done"),
 )
 BACKWARD = (
-    ("gather", 0, "own"), ("small", 0, ""), ("gather", 1, "own"), ("gather", 0, "far"),
+    ("gather", 0, "own"), ("gather", 1, "own"), ("small", 0, ""), ("gather", 0, "far"),
     ("gather", 1, "far"), ("gather", 0, "beside"), ("gather", 0, "last"), ("small", 1, ""),
     ("gather", 1, "beside"), ("gather", 1, "last"), ("small", 2, ""), ("gather", 0, "done"),
     ("handed", 0, ""), ("products", 0, ""), ("scatter", 0, "start"), ("gather", 1, "done"),

time: 75.2 us -> 74.2 us (0.987)
  Pallas kernels: 73.8 us -> 72.8 us
    pallas_call x1, Pallas kernels: 72.9 us -> 71.9 us  [shards(): pl.pallas_call(kernel, out_shape=(pltpu.VMEM((8, TILE), F32), pltpu.VMEM(...]
where the time goes in v4:
time: 74.2 us; the launch traced here: 74.1 us
  Pallas kernels  72.8 us (98%)
  between operations  1.29 us (2%)
    pallas_call x1, Pallas kernels, shards(): pl.pallas_call(kernel, out_shape=(pltpu.VMEM((8, TILE), F32), pltpu.VMEM(...  71.9 us

profile of v4, /device:TPU:0, one launch (start us, length us, event | category | flops | bytes accessed | tf_op | source)
XLA Modules:
  0.0 74.1 jit_solution(10981577080145686889)
XLA Ops:
  1.3 71.9 %graph_layer.1 = (f32[8,128]{1,0:T(8,128)S(1)}, f32[128,256]{1,0:T(8,128)S(1)}, f32[172,256]{1,0:T(8,128)S(1)}, f32[6,128,128]{2,1,0:T(8,128)S(1)}) custom-call(bf16[6,128,128]{2,1,0:T(8,128)(2,1)} %bitcast.7, bf16[1,1,96,128,128]{4,3,2,1,0:T(8,128)(2,1)} %vals_hbm.1, s32[1,96]{1,0:T(1,128)} %bitcast.9, s32[1,96]{1,0:T(1,128)} %bitcast.10, ...), custom_call_target="tpu_custom_call" | custom-call | tf_op jit(solution)/shard_map/graph_layer/pallas_call | solution.py:566
  73.2 0.9 %hand_out.1 = (f32[1]{0:T(128)}, f32[128,256]{1,0:T(8,128)}, f32[172,256]{1,0:T(8,128)}, f32[6,128,128]{2,1,0:T(8,128)}) custom-call(f32[8,128]{1,0:T(8,128)S(1)} %get-tuple-element.12.loss, f32[128,256]{1,0:T(8,128)S(1)} %get-tuple-element.13.gin, f32[172,256]{1,0:T(8,128)S(1)} %get-tuple-element.14.gout, f32[6,128,128]{2,1,0:T(8,128)S(1)} %get-tuple-element.15.gf), custom_call_target="tpu_custom_call" | custom-call | tf_op jit(solution)/shard_map/hand_out/pallas_call | solution.py:639
